TPU v7x, 128 devices: a whole 4x4x4 slice. The times are simulated.
128 devices in a mesh: rep: 4 (over y), exp: 8 (over x, core), seq: 4 (over z).
Axes of the slice: x: 4, y: 4, z: 4, core: 2. Of those that a mesh axis runs over, the one named last changes fastest.
Arguments:
- tokens: bfloat16 [16384, 1024], P(('rep', 'exp', 'seq')), may hold values from -6 to 6
- norm1_gain: bfloat16 [1024], P(('rep', 'exp', 'seq')), may hold values from 0.5 to 1.5
- w_query: bfloat16 [1024, 1024], P(('rep', 'exp', 'seq')), may hold values from -0.25 to 0.25
- w_keyval: bfloat16 [1024, 1024], P(('rep', 'exp', 'seq')), may hold values from -0.25 to 0.25
- w_output: bfloat16 [1024, 1024], P(('rep', 'exp', 'seq')), may hold values from -0.75 to 0.75
- norm2_gain: bfloat16 [1024], P(('rep', 'exp', 'seq')), may hold values from 0.5 to 1.5
- w_router: bfloat16 [1024, 32], P(('rep', 'exp', 'seq')), may hold values from -0.09375 to 0.09375
- expert_in: bfloat16 [32, 1024, 1024], P('exp'), may hold values from -0.1875 to 0.1875
- expert_out: bfloat16 [32, 512, 1024], P('exp'), may hold values from -0.5 to 0.5
- routes: int32 [16384, 8], P(('rep', 'exp', 'seq')), may hold values from 0 to 31, all different within a row; in each aligned block of 128 rows (0 to 127, 128 to 255, ...) at most 64 rows name the same one
- cotangent: bfloat16 [16384, 1024], P(('rep', 'exp', 'seq')), may hold values from -6 to 6
Outputs:
- output: bfloat16 [16384, 1024], P(('rep', 'exp', 'seq'))
- grad_tokens: float32 [16384, 1024], P(('rep', 'exp', 'seq'))
- grad_norm1: float32 [1024], P(('rep', 'exp', 'seq'))
- grad_query: float32 [1024, 1024], P(('rep', 'exp', 'seq'))
- grad_keyval: float32 [1024, 1024], P(('rep', 'exp', 'seq'))
- grad_output: float32 [1024, 1024], P(('rep', 'exp', 'seq'))
- grad_norm2: float32 [1024], P(('rep', 'exp', 'seq'))
- grad_router: float32 [1024, 32], P(('rep', 'exp', 'seq'))
- grad_expert_in: float32 [32, 1024, 1024], P('exp', ('rep', 'seq'))
- grad_expert_out: float32 [32, 512, 1024], P('exp', ('rep', 'seq'))
Inputs may be any that keep to these rules, and one draw needn't show every extreme that they name: `routes`: in the rows of one device (aligned blocks of 128 rows) no expert is named by more than 64 rows, a bound that some block reaches.
All inputs are finite; a program needn't handle non-finite values.
Results may differ from a plain program's by a relative error of at most 0.04.
Values may be sent and summed in bfloat16 or wider, within the bound.
No kernel may reach another device: no remote copies, remote signals or barrier semaphores. Data moves between devices by JAX's collectives and lax.ppermute only.
A program may use at most 192 MiB of HBM per device.

v0:
```python
import jax
import jax.numpy as jnp
from jax import lax
from jax.sharding import PartitionSpec as P

H = 16
KV = 8
HD = 64
F = 512
TOP = 8


epsilon = 1e-06


def rotation_tables(positions, head_size):
    half_size = head_size // 2
    frequencies = 10000.0 ** (-(jnp.arange(half_size, dtype=jnp.float32) * 2.0 / head_size))
    angles = positions.astype(jnp.float32)[:, None] * frequencies[None, :]
    return (jnp.cos(angles)[:, None, :], jnp.sin(angles)[:, None, :])


def rotate(vectors, cosine, sine_table):
    half_size = vectors.shape[-1] // 2
    leading = vectors[..., :half_size]
    trailing = vectors[..., half_size:]
    return jnp.concatenate(
        [leading * cosine - trailing * sine_table, trailing * cosine + leading * sine_table],
        axis=-1,
    )


def unrotate(gradient, cosine, sine_table):
    half_size = gradient.shape[-1] // 2
    leading = gradient[..., :half_size]
    trailing = gradient[..., half_size:]
    return jnp.concatenate(
        [leading * cosine + trailing * sine_table, trailing * cosine - leading * sine_table],
        axis=-1,
    )


def rms_forward(vectors, gain_vector):
    inverse = lax.rsqrt(jnp.mean(vectors * vectors, axis=-1, keepdims=True) + epsilon)
    return (vectors * inverse * gain_vector, inverse)


def rms_backward(vectors, inverse, gain_vector, grad_scaled):
    grad_gain = jnp.sum(grad_scaled * vectors * inverse, axis=0)
    grad_hidden = grad_scaled * gain_vector
    grad_input = inverse * grad_hidden - vectors * inverse * inverse * inverse * jnp.mean(
        grad_hidden * vectors, axis=-1, keepdims=True
    )
    return (grad_gain, grad_input)


def local(
    tokens,
    norm1_gain,
    w_query,
    w_keyval,
    w_output,
    norm2_gain,
    w_router,
    expert_in,
    expert_out,
    routes,
    cotangent,
):
    f32 = jnp.float32
    bf16 = jnp.bfloat16
    tok_rows = tokens.shape[0]
    width = tokens.shape[1]
    groups = H // KV
    score_scale = HD ** (-0.5)
    dense_shards = (norm1_gain, w_query, w_keyval, w_output, norm2_gain, w_router)
    gain_one, query_all, keyval_all, output_all, gain_two, router_all = (
        lax.all_gather(dense_shards[0], ("rep", "exp", "seq"), axis=0, tiled=True),
        lax.all_gather(dense_shards[1], ("rep", "exp", "seq"), axis=0, tiled=True),
        lax.all_gather(dense_shards[2], ("rep", "exp", "seq"), axis=0, tiled=True),
        lax.all_gather(dense_shards[3], ("rep", "exp", "seq"), axis=0, tiled=True),
        lax.all_gather(dense_shards[4], ("rep", "exp", "seq"), axis=0, tiled=True),
        lax.all_gather(dense_shards[5], ("rep", "exp", "seq"), axis=0, tiled=True),
    )
    token_f = tokens.astype(f32)
    gain_one_f = gain_one.astype(f32)
    gain_two_f = gain_two.astype(f32)
    hidden1_f, inverse_one = rms_forward(token_f, gain_one_f)
    hidden1 = hidden1_f.astype(bf16)
    query_raw = jnp.dot(hidden1, query_all, preferred_element_type=f32)
    keyval_raw = jnp.dot(hidden1, keyval_all, preferred_element_type=f32)
    first_position = lax.axis_index(("exp", "seq")) * tok_rows
    positions = first_position + jnp.arange(tok_rows, dtype=jnp.int32)
    last_query = first_position + tok_rows - 1
    cosine, sine_table = rotation_tables(positions, HD)
    queries = rotate(query_raw.reshape(tok_rows, H, HD), cosine, sine_table).astype(bf16)
    key_rows = rotate(
        keyval_raw[:, : KV * HD].reshape(tok_rows, KV, HD), cosine, sine_table
    ).astype(bf16)
    value_rows = keyval_raw[:, KV * HD :].reshape(tok_rows, KV, HD).astype(bf16)
    query_groups = queries.reshape(tok_rows, KV, groups, HD)
    initial = (
        jnp.full((KV, groups, tok_rows), -1e30, f32),
        jnp.zeros((KV, groups, tok_rows), f32),
        jnp.zeros((KV, groups, tok_rows, HD), f32),
    )
    running = initial
    key_piece = lax.all_gather(key_rows, ("exp", "seq"), axis=0, tiled=True)
    value_piece = lax.all_gather(value_rows, ("exp", "seq"), axis=0, tiled=True)
    piece_rows = key_piece.shape[0]
    fold_block_rows = 512
    count_blocks = piece_rows // fold_block_rows
    key_blocks = key_piece.reshape(count_blocks, fold_block_rows, KV, HD)
    value_blocks = value_piece.reshape(count_blocks, fold_block_rows, KV, HD)
    starts = jnp.arange(count_blocks, dtype=jnp.int32) * fold_block_rows

    def key_step(current, blocks):
        key_block, value_block, block_start = blocks

        def update(current):
            running_max, running_sum, running_acc = current
            scores = (
                jnp.einsum("tkgd,nkd->kgtn", query_groups, key_block, preferred_element_type=f32)
                * score_scale
            )
            allowed = (
                positions[:, None]
                >= (block_start + jnp.arange(fold_block_rows, dtype=jnp.int32))[None, :]
            )
            scores = jnp.where(allowed, scores, -1e30)
            new_max = jnp.maximum(running_max, jnp.max(scores, axis=-1))
            weights = jnp.where(allowed, jnp.exp(scores - new_max[..., None]), 0.0)
            shrink = jnp.exp(running_max - new_max)
            new_sum = running_sum * shrink + jnp.sum(weights, axis=-1)
            new_acc = running_acc * shrink[..., None] + jnp.einsum(
                "kgtn,nkd->kgtd", weights.astype(bf16), value_block, preferred_element_type=f32
            )
            return (new_max, new_sum, new_acc)

        return (
            lax.cond(block_start <= last_query, update, lambda unchanged: unchanged, current),
            None,
        )

    running, _ = lax.scan(key_step, running, (key_blocks, value_blocks, starts))
    run_max, run_sum, run_acc = running
    attended_f = run_acc / run_sum[..., None]
    log_total = run_max + jnp.log(run_sum)
    attended_rows = attended_f.transpose(2, 0, 1, 3)
    attended = attended_rows.reshape(tok_rows, H * HD).astype(bf16)
    middle = token_f + jnp.dot(attended, output_all, preferred_element_type=f32)
    hidden2_f, inverse_two = rms_forward(middle, gain_two_f)
    hidden2 = hidden2_f.astype(bf16)
    logits = jnp.dot(hidden2, router_all, preferred_element_type=f32)
    experts = router_all.shape[1]
    chosen_hot = (routes[:, :, None] == jnp.arange(experts, dtype=jnp.int32)[None, None, :]).astype(
        f32
    )
    chosen = jnp.sum(chosen_hot * logits[:, None, :], axis=-1)
    gate_weights = jax.nn.softmax(chosen, axis=-1)
    route_count = tok_rows * TOP
    capacity = min(tok_rows, 2 * tok_rows * TOP // experts)
    flat_routes = routes.reshape(route_count)
    route_hot = (flat_routes[:, None] == jnp.arange(experts, dtype=jnp.int32)[None, :]).astype(
        jnp.int32
    )
    slot_ranks = jnp.sum(jnp.cumsum(route_hot, axis=0) * route_hot, axis=1) - 1
    slot_index = flat_routes * capacity + slot_ranks
    owners = (
        jnp.full((experts * capacity,), route_count, jnp.int32)
        .at[slot_index]
        .set(jnp.arange(route_count, dtype=jnp.int32))
    )
    owner_tokens = owners // TOP
    peer_count = lax.axis_size("exp")
    local_experts = expert_in.shape[0]
    hidden2_ext = jnp.concatenate([hidden2, jnp.zeros((1, width), bf16)], axis=0)
    outgoing = hidden2_ext[owner_tokens].reshape(peer_count, local_experts, capacity, width)
    arrived = lax.all_to_all(outgoing, "exp", split_axis=0, concat_axis=0, tiled=True)
    projected = jnp.einsum("sjcd,jdf->sjcf", arrived, expert_in, preferred_element_type=f32)
    active = (jax.nn.silu(projected[..., :F]) * projected[..., F:]).astype(bf16)
    produced = jnp.einsum("sjcf,jfd->sjcd", active, expert_out, preferred_element_type=f32).astype(
        bf16
    )
    produced, arrived_rows = (produced, arrived)
    returned = lax.all_to_all(produced, "exp", split_axis=0, concat_axis=0, tiled=True)
    route_values = (
        returned.reshape(experts * capacity, width)[slot_index]
        .reshape(tok_rows, TOP, width)
        .astype(f32)
    )
    mixture = jnp.sum(gate_weights[:, :, None] * route_values, axis=1)
    output = (middle + mixture).astype(bf16)
    gain_one, query_all, keyval_all, output_all, gain_two, router_all = (
        lax.all_gather(dense_shards[0], ("rep", "exp", "seq"), axis=0, tiled=True),
        lax.all_gather(dense_shards[1], ("rep", "exp", "seq"), axis=0, tiled=True),
        lax.all_gather(dense_shards[2], ("rep", "exp", "seq"), axis=0, tiled=True),
        lax.all_gather(dense_shards[3], ("rep", "exp", "seq"), axis=0, tiled=True),
        lax.all_gather(dense_shards[4], ("rep", "exp", "seq"), axis=0, tiled=True),
        lax.all_gather(dense_shards[5], ("rep", "exp", "seq"), axis=0, tiled=True),
    )
    gain_one_f = gain_one.astype(f32)
    gain_two_f = gain_two.astype(f32)
    grad_final = cotangent.astype(f32)
    grad_gates = jnp.sum(grad_final[:, None, :] * route_values, axis=-1)
    gate_ext = jnp.concatenate([gate_weights.reshape(route_count), jnp.zeros((1,), f32)], axis=0)
    cotangent_ext = jnp.concatenate([cotangent, jnp.zeros((1, width), bf16)], axis=0)
    slot_grads = (
        (gate_ext[owners][:, None] * cotangent_ext[owner_tokens].astype(f32))
        .astype(bf16)
        .reshape(peer_count, local_experts, capacity, width)
    )
    arrived_in, arrived_grad = (
        lax.all_to_all(outgoing, "exp", split_axis=0, concat_axis=0, tiled=True),
        lax.all_to_all(slot_grads, "exp", split_axis=0, concat_axis=0, tiled=True),
    )
    projected = jnp.einsum("sjcd,jdf->sjcf", arrived_in, expert_in, preferred_element_type=f32)
    gate_half = projected[..., :F]
    up_half = projected[..., F:]
    sigmoid_gate = jax.nn.sigmoid(gate_half)
    silu_gate = gate_half * sigmoid_gate
    active = (silu_gate * up_half).astype(bf16)
    grad_active = jnp.einsum("sjcd,jfd->sjcf", arrived_grad, expert_out, preferred_element_type=f32)
    grad_gate_half = grad_active * up_half * sigmoid_gate * (1.0 + gate_half * (1.0 - sigmoid_gate))
    grad_projected = jnp.concatenate([grad_gate_half, grad_active * silu_gate], axis=-1).astype(
        bf16
    )
    grad_rows = jnp.einsum(
        "sjcf,jdf->sjcd", grad_projected, expert_in, preferred_element_type=f32
    ).astype(bf16)
    grad_in_local = jnp.einsum(
        "sjcd,sjcf->jdf", arrived_in, grad_projected, preferred_element_type=f32
    )
    grad_out_local = jnp.einsum("sjcf,sjcd->jfd", active, arrived_grad, preferred_element_type=f32)
    grad_returned = lax.all_to_all(grad_rows, "exp", split_axis=0, concat_axis=0, tiled=True)
    grad_hidden2 = jnp.sum(
        grad_returned.reshape(experts * capacity, width)[slot_index]
        .reshape(tok_rows, TOP, width)
        .astype(f32),
        axis=1,
    )
    grad_chosen = gate_weights * (
        grad_gates - jnp.sum(gate_weights * grad_gates, axis=-1, keepdims=True)
    )
    grad_logits = jnp.sum(chosen_hot * grad_chosen[:, :, None], axis=1).astype(bf16)
    grad_hidden2 = grad_hidden2 + jnp.dot(grad_logits, router_all.T, preferred_element_type=f32)
    grad_router = jnp.dot(hidden2.T, grad_logits, preferred_element_type=f32)
    grad_gain_two, grad_middle_norm = rms_backward(middle, inverse_two, gain_two_f, grad_hidden2)
    grad_middle = grad_final + grad_middle_norm
    grad_branch = grad_middle.astype(bf16)
    grad_output = jnp.dot(attended.T, grad_branch, preferred_element_type=f32)
    grad_attended = jnp.dot(grad_branch, output_all.T, preferred_element_type=f32).astype(bf16)
    grad_attended_groups = grad_attended.reshape(tok_rows, KV, groups, HD)
    row_delta = jnp.sum(grad_attended_groups.astype(f32) * attended_rows, axis=-1).transpose(
        1, 2, 0
    )
    keys_all, values_all = (
        lax.all_gather(key_rows, ("exp", "seq"), axis=0, tiled=True),
        lax.all_gather(value_rows, ("exp", "seq"), axis=0, tiled=True),
    )
    length = keys_all.shape[0]
    block_rows = 512
    count_blocks = length // block_rows
    block_starts = jnp.arange(count_blocks, dtype=jnp.int32) * block_rows

    def back_step(grad_queries, blocks):
        key_block, value_block, block_start = blocks

        def compute(grad_queries):
            scores = (
                jnp.einsum("tkgd,nkd->kgtn", query_groups, key_block, preferred_element_type=f32)
                * score_scale
            )
            allowed = (
                positions[:, None]
                >= (block_start + jnp.arange(block_rows, dtype=jnp.int32))[None, :]
            )
            probabilities = jnp.where(allowed, jnp.exp(scores - log_total[..., None]), 0.0)
            grad_probs = jnp.einsum(
                "tkgd,nkd->kgtn", grad_attended_groups, value_block, preferred_element_type=f32
            )
            grad_scores = (probabilities * (grad_probs - row_delta[..., None])).astype(bf16)
            new_grad = (
                grad_queries
                + jnp.einsum("kgtn,nkd->tkgd", grad_scores, key_block, preferred_element_type=f32)
                * score_scale
            )
            grad_key = (
                jnp.einsum("kgtn,tkgd->nkd", grad_scores, query_groups, preferred_element_type=f32)
                * score_scale
            )
            grad_value = jnp.einsum(
                "kgtn,tkgd->nkd",
                probabilities.astype(bf16),
                grad_attended_groups,
                preferred_element_type=f32,
            )
            return (
                new_grad,
                jnp.concatenate(
                    [
                        grad_key.reshape(block_rows, KV * HD),
                        grad_value.reshape(block_rows, KV * HD),
                    ],
                    axis=-1,
                ),
            )

        def skipped(grad_queries):
            return (grad_queries, jnp.zeros((block_rows, 2 * KV * HD), f32))

        return lax.cond(block_start <= last_query, compute, skipped, grad_queries)

    grad_queries, key_terms = lax.scan(
        back_step,
        jnp.zeros((tok_rows, KV, groups, HD), f32),
        (
            keys_all.reshape(count_blocks, block_rows, KV, HD),
            values_all.reshape(count_blocks, block_rows, KV, HD),
            block_starts,
        ),
    )
    key_grads = lax.psum_scatter(
        key_terms.reshape(length, 2 * KV * HD).astype(jnp.bfloat16),
        ("exp", "seq"),
        scatter_dimension=0,
        tiled=True,
    ).astype(jnp.float32)
    grad_query_raw = (
        unrotate(grad_queries.reshape(tok_rows, H, HD), cosine, sine_table)
        .reshape(tok_rows, H * HD)
        .astype(bf16)
    )
    grad_key_raw = unrotate(
        key_grads[:, : KV * HD].reshape(tok_rows, KV, HD), cosine, sine_table
    ).reshape(tok_rows, KV * HD)
    grad_keyval_raw = jnp.concatenate([grad_key_raw, key_grads[:, KV * HD :]], axis=-1).astype(bf16)
    grad_hidden1 = jnp.dot(grad_query_raw, query_all.T, preferred_element_type=f32) + jnp.dot(
        grad_keyval_raw, keyval_all.T, preferred_element_type=f32
    )
    grad_query = jnp.dot(hidden1.T, grad_query_raw, preferred_element_type=f32)
    grad_keyval = jnp.dot(hidden1.T, grad_keyval_raw, preferred_element_type=f32)
    grad_gain_one, grad_token_norm = rms_backward(token_f, inverse_one, gain_one_f, grad_hidden1)
    grad_tokens = grad_middle + grad_token_norm
    dense_summed = (
        lax.psum_scatter(grad_gain_one, ("rep", "exp", "seq"), scatter_dimension=0, tiled=True),
        lax.psum_scatter(grad_query, ("rep", "exp", "seq"), scatter_dimension=0, tiled=True),
        lax.psum_scatter(grad_keyval, ("rep", "exp", "seq"), scatter_dimension=0, tiled=True),
        lax.psum_scatter(grad_output, ("rep", "exp", "seq"), scatter_dimension=0, tiled=True),
        lax.psum_scatter(grad_gain_two, ("rep", "exp", "seq"), scatter_dimension=0, tiled=True),
        lax.psum_scatter(grad_router, ("rep", "exp", "seq"), scatter_dimension=0, tiled=True),
    )
    expert_summed = (
        lax.psum_scatter(
            grad_in_local.astype(jnp.bfloat16), ("rep", "seq"), scatter_dimension=1, tiled=True
        ).astype(jnp.float32),
        lax.psum_scatter(
            grad_out_local.astype(jnp.bfloat16), ("rep", "seq"), scatter_dimension=1, tiled=True
        ).astype(jnp.float32),
    )
    return (
        output,
        grad_tokens,
        dense_summed[0],
        dense_summed[1],
        dense_summed[2],
        dense_summed[3],
        dense_summed[4],
        dense_summed[5],
        expert_summed[0],
        expert_summed[1],
    )


def solution(mesh):
    placed = (
        P(("rep", "exp", "seq"), None),
        P(("rep", "exp", "seq")),
        P(("rep", "exp", "seq"), None),
        P(("rep", "exp", "seq"), None),
        P(("rep", "exp", "seq"), None),
        P(("rep", "exp", "seq")),
        P(("rep", "exp", "seq"), None),
        P("exp", None, None),
        P("exp", None, None),
        P(("rep", "exp", "seq"), None),
        P(("rep", "exp", "seq"), None),
    )
    return jax.shard_map(
        local,
        mesh=mesh,
        in_specs=placed,
        out_specs=(
            P(("rep", "exp", "seq"), None),
            P(("rep", "exp", "seq"), None),
            P(("rep", "exp", "seq")),
            P(("rep", "exp", "seq"), None),
            P(("rep", "exp", "seq"), None),
            P(("rep", "exp", "seq"), None),
            P(("rep", "exp", "seq")),
            P(("rep", "exp", "seq"), None),
            P("exp", ("rep", "seq"), None),
            P("exp", ("rep", "seq"), None),
        ),
        check_vma=False,
    )
```

profile of v0, /device:TPU:0, one launch (start us, length us, event | category | flops | bytes accessed | tf_op | source)
XLA Modules:
  0.0 3088.6 jit_solution(1976069568806140065)
XLA Ops:
  10.4 68.7 %all-reduce.8 = (bf16[1024]{0:T(1024)(128)(2,1)S(1)}, bf16[1024]{0:T(1024)(128)(2,1)S(1)}) all-reduce(bf16[1024]{0:T(1024)(128)(2,1)S(1)} %dynamic-update-slice, bf16[1024]{0:T(1024)(128)(2,1)S(1)} %dynamic-update-slice.1), channel_id=1, replica_groups=mesh['rep'=4,'exp'=8,'seq'=4] {'rep','exp','seq'}, use_global_device_ids=true, to_apply=%add.2 | all-reduce | flops 2048 | bytes 8192
  80.5 2.2 fusion.118
  85.3 9.0 reduce-window.6
  95.1 4.3 scatter_custom_fusion
  99.5 44.9 %all-gather.10.cloned.1.call-done = bf16[1024,1024]{1,0:T(8,128)(2,1)} async-done(((bf16[8,1024]{1,0:T(8,128)(2,1)}), bf16[1024,1024]{1,0:T(8,128)(2,1)}) %all-gather.10.cloned.1.call-update) | async-done | bytes 2097168 | tf_op jit(solution)/shard_map/all_gather | solution.py:79
  144.4 2.6 fusion.116
  147.1 46.9 %all-gather.8.cloned.1.call-done = bf16[4096,8,64]{0,2,1:T(8,128)(2,1)} async-done(((bf16[128,8,64]{0,2,1:T(8,128)(2,1)}), bf16[4096,8,64]{0,2,1:T(8,128)(2,1)}) %all-gather.8.cloned.1.call-update) | async-done | bytes 4194320 | tf_op jit(solution)/shard_map/all_gather | solution.py:108
  194.0 4.8 copy.197
  198.8 46.7 %all-gather.12.cloned.1.call-done = bf16[4096,8,64]{0,2,1:T(8,128)(2,1)} async-done(((bf16[128,8,64]{0,2,1:T(8,128)(2,1)}), bf16[4096,8,64]{0,2,1:T(8,128)(2,1)}) %all-gather.12.cloned.1.call-update) | async-done | bytes 4194320 | tf_op jit(solution)/shard_map/all_gather | solution.py:109
  245.5 4.8 copy.196
  250.3 16.2 while.31
  251.6 6.0 conditional.6
  252.4 1.9 fusion.4
  255.3 2.2 fusion.10
  266.6 46.4 %all-gather.14.cloned.1.call-done = bf16[1024,1024]{1,0:T(8,128)(2,1)} async-done(((bf16[8,1024]{1,0:T(8,128)(2,1)}), bf16[1024,1024]{1,0:T(8,128)(2,1)}) %all-gather.14.cloned.1.call-update) | async-done | bytes 2097168 | tf_op jit(solution)/shard_map/all_gather | solution.py:81
  313.0 2.1 multiply_reduce_fusion.2
  315.3 9.6 gather_fusion
  324.9 4.7 all-to-all-start
  329.6 9.7 gather_fusion.3
  339.3 84.3 %all_gather.39 = bf16[1024,32]{1,0:T(8,128)(2,1)S(1)} all-gather(bf16[8,32]{1,0:T(8,128)(2,1)S(1)} %copy-done.23), channel_id=1, replica_groups=mesh['rep'=4,'exp'=8,'seq'=4] {'rep','exp','seq'}, dimensions={0}, use_global_device_ids=true | all-gather | bytes 66048 | tf_op jit(solution)/shard_map/all_gather | solution.py:83
  424.2 11.8 gather_fusion.2
  436.1 4.9 fusion.49
  441.0 4.6 all-to-all-start.2
  445.5 12.4 fusion.70
  457.9 37.3 %all-to-all-done.2 = bf16[8,4,64,1024]{3,2,1,0:T(8,128)(2,1)} async-done(((bf16[8,4,64,1024]{3,2,1,0:T(8,128)(2,1)}), bf16[8,4,64,1024]{3,2,1,0:T(8,128)(2,1)}, u32[]{:S(2)}, u32[]{:S(2)}) %all-to-all-start.2) | async-done | bytes 4194336 | tf_op jit(solution)/shard_map/all_to_all | solution.py:215
  495.2 11.8 fusion.58
  507.0 2.3 convert_bitcast_fusion.1
  509.4 2.4 copy.132
  511.8 15.7 all-to-all-start.1
  527.5 11.1 convert_bitcast_fusion
  538.6 4.9 copy.135
  543.5 33.4 %all-to-all-done.1 = bf16[8,4,64,1024]{3,2,1,0:T(8,128)(2,1)} async-done(((bf16[8,4,64,1024]{3,2,1,0:T(8,128)(2,1)}), bf16[8,4,64,1024]{3,2,1,0:T(8,128)(2,1)}, u32[]{:S(2)}, u32[]{:S(2)}) %all-to-all-start.1) | async-done | bytes 4194336 | tf_op jit(solution)/shard_map/all_to_all | solution.py:186
  576.9 4.6 all-to-all-start.3
  582.4 7.7 gather_fusion.1
  590.1 3.5 fusion.55
  593.8 37.4 %all-to-all-done.3 = bf16[8,4,64,1024]{3,2,1,0:T(8,128)(2,1)} async-done(((bf16[8,4,64,1024]{3,2,1,0:T(8,128)(2,1)}), bf16[8,4,64,1024]{3,2,1,0:T(8,128)(2,1)}, u32[]{:S(2)}, u32[]{:S(2)}) %all-to-all-start.3) | async-done | bytes 4194336 | tf_op jit(solution)/shard_map/all_to_all | solution.py:235
  631.2 7.7 gather_fusion.4
  638.9 1.4 convert_reduce_fusion
  644.5 33.1 %while.32 = (s32[]{:T(128)}, f32[128,8,2,64]{0,3,2,1:T(8,128)S(1)}, bf16[8,512,1024]{2,1,0:T(8,128)(2,1)}, s32[8]{0:T(128)S(1)}, s32[]{:T(128)}, /*index=5*/bf16...) while((s32[]{:T(128)}, f32[128,8,2,64]{0,3,2,1:T(8,128)S(1)}, ...), condition=%wide.region_25.26_spmd.clone, body=%wide.region_22.25_spmd.clone.sunk | while | flops 684524160 | bytes 30114056 | solution.py:314
  645.8 9.5 conditional.7
  645.8 1.8 fusion.39
  648.4 2.6 fusion.24
  651.8 1.9 fusion.28
  653.7 1.6 fusion.36
  655.8 1.1 constant_dynamic-update-slice_fusion.2
  679.9 6.5 bitcast_convert_fusion.1
  686.5 1.5 copy-done.27
  688.0 10.7 bitcast_convert_fusion
  699.7 2.7 fusion.114
  702.5 2.7 fusion.96
  705.2 126.9 %reduce-scatter.7.cloned.1.call-done = bf16[128,1024]{1,0:T(8,128)(2,1)} async-done(((bf16[4096,1024]{1,0:T(8,128)(2,1)}), bf16[128,1024]{1,0:T(8,128)(2,1)}) %reduce-scatter.7.cloned.1.call-update) | async-done | bytes 262160 | tf_op jit(solution)/shard_map/reduce_scatter | solution.py:323
  833.5 2.8 fusion.93
  836.3 3.4 fusion.121
  839.6 142.4 %all-reduce.11.cloned.1.call-done = f32[1024,32]{1,0:T(8,128)} async-done(((f32[1024,32]{1,0:T(8,128)}), f32[1024,32]{1,0:T(8,128)}) %all-reduce.11.cloned.1.call-update) | async-done | bytes 131088
  982.0 1.3 constant_dynamic-slice_fusion
  983.3 79.2 %reduce-scatter.17.cloned.1.call-done = bf16[4,32,1024]{2,1,0:T(8,128)(2,1)} async-done(((bf16[4,512,1024]{2,1,0:T(8,128)(2,1)}), bf16[4,32,1024]{2,1,0:T(8,128)(2,1)}) %reduce-scatter.17.cloned.1.call-update) | async-done | bytes 262160 | tf_op jit(solution)/shard_map/reduce_scatter | solution.py:357
  1062.5 1.8 convert_element_type.184
  1064.3 2.6 fusion.91
  1066.9 65.1 %all-reduce.7 = (f32[1024]{0:T(1024)S(1)}, f32[1024]{0:T(1024)S(1)}) all-reduce(f32[1024]{0:T(1024)S(1)} %get-tuple-element.465, f32[1024]{0:T(1024)S(1)} %get-tuple-element.463), channel_id=3, replica_groups=mesh['rep'=4,'exp'=8,'seq'=4] {'rep','exp','seq'}, use_global_device_ids=true, to_apply=%region_29.30.clone | all-reduce | flops 2048 | bytes 16384
  1134.8 16.2 reduce-scatter.15.cloned.1.call-done
  1151.0 2.1 convert_element_type.182
  1153.1 644.7 %reduce-scatter.9.cloned.1.call-done = f32[8,1024]{1,0:T(8,128)} async-done(((f32[1024,1024]{1,0:T(8,128)}), f32[8,1024]{1,0:T(8,128)}) %reduce-scatter.9.cloned.1.call-update) | async-done | bytes 32784 | tf_op jit(solution)/shard_map/reduce_scatter | solution.py:347
  1797.9 641.8 %reduce-scatter.13.cloned.1.call-done = f32[8,1024]{1,0:T(8,128)} async-done(((f32[1024,1024]{1,0:T(8,128)}), f32[8,1024]{1,0:T(8,128)}) %reduce-scatter.13.cloned.1.call-update) | async-done | bytes 32784 | tf_op jit(solution)/shard_map/reduce_scatter | solution.py:349
  2439.6 641.7 %reduce-scatter.11.cloned.1.call-done = f32[8,1024]{1,0:T(8,128)} async-done(((f32[1024,1024]{1,0:T(8,128)}), f32[8,1024]{1,0:T(8,128)}) %reduce-scatter.11.cloned.1.call-update) | async-done | bytes 32784 | tf_op jit(solution)/shard_map/reduce_scatter | solution.py:348
  (243 shorter events, 47.3 us)
Async XLA Ops:
  7.2 137.2 %copy-start = (bf16[128,1024]{1,0:T(8,128)(2,1)S(1)}, bf16[128,1024]{1,0:T(8,128)(2,1)}, u32[]{:S(2)}) copy-start(bf16[128,1024]{1,0:T(8,128)(2,1)} %param.19) | copy-start | bytes 786436
  7.2 77.8 %copy-start.20 = (s32[128,8]{0,1:T(8,128)S(1)}, s32[128,8]{0,1:T(8,128)}, u32[]{:S(2)}) copy-start(s32[128,8]{0,1:T(8,128)} %param.28) | copy-start | bytes 12292
  7.2 73.3 %all-gather.6.cloned.1.call-start = ((), (), s32[]{:S(2)}) async-start(), calls=%async_computation.10 | async-start | bytes 2113536 | tf_op jit(solution)/shard_map/all_gather | solution.py:80
  7.9 136.5 %all-gather.10.cloned.1.call-start = ((), (), s32[]{:S(2)}) async-start(), calls=%async_computation.12 | async-start | bytes 2113536 | tf_op jit(solution)/shard_map/all_gather | solution.py:79
  8.7 185.3 %all-gather.8.cloned.1.call-start = ((), (), s32[]{:S(2)}) async-start(), calls=%async_computation.11 | async-start | bytes 4325376 | tf_op jit(solution)/shard_map/all_gather | solution.py:108
  79.1 67.8 %copy-start.18 = (f32[1024]{0:T(1024)}, f32[1024]{0:T(1024)S(1)}, u32[]{:S(2)}) copy-start(f32[1024]{0:T(1024)S(1)} %convert_element_type.151) | copy-start | bytes 12292
  80.3 66.7 %copy-start.21 = (f32[128]{0:T(128)}, f32[128]{0:T(128)S(1)}, u32[]{:S(2)}) copy-start(f32[128]{0:T(128)S(1)} %add_rsqrt_fusion.1) | copy-start | bytes 1540
  80.4 66.6 %copy-start.14 = (f32[128,32]{0,1:T(8,128)}, f32[128,32]{0,1:T(8,128)S(1)}, u32[]{:S(2)}) copy-start(f32[128,32]{0,1:T(8,128)S(1)} %get-tuple-element.536) | copy-start | bytes 49156
  80.4 66.6 %copy-start.16 = (f32[128,32]{0,1:T(8,128)}, f32[128,32]{0,1:T(8,128)S(1)}, u32[]{:S(2)}) copy-start(f32[128,32]{0,1:T(8,128)S(1)} %get-tuple-element.537) | copy-start | bytes 49156
  83.6 161.9 %all-gather.12.cloned.1.call-start = ((), (), s32[]{:S(2)}) async-start(), calls=%async_computation.13 | async-start | bytes 4325376 | tf_op jit(solution)/shard_map/all_gather | solution.py:109
  84.4 228.6 %all-gather.14.cloned.1.call-start = ((), (), s32[]{:S(2)}) async-start(), calls=%async_computation.14 | async-start | bytes 2113536 | tf_op jit(solution)/shard_map/all_gather | solution.py:81
  266.5 48.6 %copy-start.4 = (f32[8,2,128,64]{2,3,1,0:T(8,128)}, f32[8,2,128,64]{2,3,1,0:T(8,128)S(1)}, u32[]{:S(2)}) copy-start(f32[8,2,128,64]{2,3,1,0:T(8,128)S(1)} %get-tuple-element.295) | copy-start | bytes 1572868
  266.6 48.6 %copy-start.10 = (bf16[128,8,2,64]{0,3,2,1:T(8,128)(2,1)}, bf16[128,8,2,64]{0,3,2,1:T(8,128)(2,1)S(1)}, u32[]{:S(2)}) copy-start(bf16[128,8,2,64]{0,3,2,1:T(8,128)(2,1)S(1)} %bitcast_convert_fusion.2) | copy-start | bytes 786436
  315.3 108.4 %copy-start.6 = (bf16[128,1024]{1,0:T(8,128)(2,1)}, bf16[128,1024]{1,0:T(8,128)(2,1)S(1)}, u32[]{:S(2)}) copy-start(bf16[128,1024]{1,0:T(8,128)(2,1)S(1)} %multiply_convert_fusion.1) | copy-start | bytes 786436
  324.9 4.7 copy-start.8
  324.9 116.1 %all-to-all-start = ((bf16[8,4,64,1024]{3,2,1,0:T(8,128)(2,1)}), bf16[8,4,64,1024]{3,2,1,0:T(8,128)(2,1)}, u32[]{:S(2)}, u32[]{:S(2)}) async-start(bf16[8,4,64,1024]{3,2,1,0:T(8,128)(2,1)} %bitcast.221), calls=%async_computation | async-start | bytes 8388608 | tf_op jit(solution)/shard_map/all_to_all | solution.py:179
  329.6 9.7 copy-start.23
  441.0 54.3 %all-to-all-start.2 = ((bf16[8,4,64,1024]{3,2,1,0:T(8,128)(2,1)}), bf16[8,4,64,1024]{3,2,1,0:T(8,128)(2,1)}, u32[]{:S(2)}, u32[]{:S(2)}) async-start(bf16[8,4,64,1024]{3,2,1,0:T(8,128)(2,1)} %fusion.49), calls=%async_computation.2 | async-start | bytes 8388608 | tf_op jit(solution)/shard_map/all_to_all | solution.py:215
  495.2 11.8 copy-start.24
  507.0 2.4 copy-start.25
  511.8 65.1 %all-to-all-start.1 = ((bf16[8,4,64,1024]{3,2,1,0:T(8,128)(2,1)}), bf16[8,4,64,1024]{3,2,1,0:T(8,128)(2,1)}, u32[]{:S(2)}, u32[]{:S(2)}) async-start(bf16[8,4,64,1024]{3,2,1,0:T(8,128)(2,1)} %copy.132), calls=%async_computation.1 | async-start | bytes 8388608 | tf_op jit(solution)/shard_map/all_to_all | solution.py:186
  576.9 54.2 %all-to-all-start.3 = ((bf16[8,4,64,1024]{3,2,1,0:T(8,128)(2,1)}), bf16[8,4,64,1024]{3,2,1,0:T(8,128)(2,1)}, u32[]{:S(2)}, u32[]{:S(2)}) async-start(bf16[8,4,64,1024]{3,2,1,0:T(8,128)(2,1)} %copy.135), calls=%async_computation.3 | async-start | bytes 8388608 | tf_op jit(solution)/shard_map/all_to_all | solution.py:235
  581.5 250.6 %reduce-scatter.7.cloned.1.call-start = ((), (), s32[]{:S(2)}) async-start(), calls=%async_computation.15 | async-start | bytes 8650752 | tf_op jit(solution)/shard_map/reduce_scatter | solution.py:323
  638.9 1.9 copy-start.9
  638.9 1.9 copy-start.12
  638.9 2.8 copy-start.3
  640.3 3.1 copy-start.5
  677.6 0.9 copy-start.7
  677.6 2.3 copy-start.26
  677.6 304.4 %all-reduce.11.cloned.1.call-start = ((), (), s32[]{:S(2)}) async-start(), calls=%async_computation.21 | async-start | bytes 1048576
  679.6 382.9 %reduce-scatter.17.cloned.1.call-start = ((), (), s32[]{:S(2)}) async-start(), calls=%async_computation.20 | async-start | bytes 4456448 | tf_op jit(solution)/shard_map/reduce_scatter | solution.py:357
  686.4 1.6 copy-start.27
  686.5 464.6 %reduce-scatter.15.cloned.1.call-start = ((), (), s32[]{:S(2)}) async-start(), calls=%async_computation.19 | async-start | bytes 8912896 | tf_op jit(solution)/shard_map/reduce_scatter | solution.py:354
  698.7 0.7 copy-start.15
  698.7 0.7 copy-start.17
  698.7 1.0 copy-start.1
  698.7 1.0 copy-start.19
  698.7 1.0 copy-start.22
  698.7 1099.2 %reduce-scatter.9.cloned.1.call-start = ((), (), s32[]{:S(2)}) async-start(), calls=%async_computation.16 | async-start | bytes 4227072 | tf_op jit(solution)/shard_map/reduce_scatter | solution.py:347
  699.7 2.8 copy-start.11
  702.4 1737.2 %reduce-scatter.13.cloned.1.call-start = ((), (), s32[]{:S(2)}) async-start(), calls=%async_computation.18 | async-start | bytes 4227072 | tf_op jit(solution)/shard_map/reduce_scatter | solution.py:349
  705.2 2376.2 %reduce-scatter.11.cloned.1.call-start = ((), (), s32[]{:S(2)}) async-start(), calls=%async_computation.17 | async-start | bytes 4227072 | tf_op jit(solution)/shard_map/reduce_scatter | solution.py:348
  833.5 2.8 copy-start.13
  836.2 228.0 %copy-start.2 = (bf16[1024,1024]{1,0:T(8,128)(2,1)S(1)}, bf16[1024,1024]{1,0:T(8,128)(2,1)}, u32[]{:S(2)}) copy-start(bf16[1024,1024]{1,0:T(8,128)(2,1)} %all-gather.6.cloned.1.call-done) | copy-start | bytes 6291460
Sparse Core Ops, SparseCore 0:
  11.0 67.6 all-gather.5
  81.7 62.6 all-gather.9
  147.2 46.8 all-gather.7
  196.6 48.7 all-gather.11
  248.3 64.6 all-gather.13
  677.8 154.3 reduce-scatter.6
  838.2 143.8 all-reduce.10
  985.4 77.0 reduce-scatter.16
  1066.3 84.7 reduce-scatter.14
  1153.9 643.9 reduce-scatter.8
  1800.8 638.7 reduce-scatter.12
  2442.5 638.7 reduce-scatter.10
where the time goes:
time: 3100 us; the launch traced here: 3090 us
  waiting for transfers between devices  2590 us (84%)
  blocking collectives  218 us (7%)
  local copies, waits for them, and re-layouts  101 us (3%)
  matrix products  91.1 us (3%)
  other arithmetic  33.6 us (1%)
    reduce_scatter x1, waiting for transfers between devices, local(): lax.psum_scatter(grad_query, ('rep', 'exp', 'seq'), scatter_dimension=0,...  645 us
    reduce_scatter x1, waiting for transfers between devices, local(): lax.psum_scatter(grad_output, ('rep', 'exp', 'seq'), scatter_dimension=0,...  642 us
    reduce_scatter x1, waiting for transfers between devices, local(): lax.psum_scatter(grad_keyval, ('rep', 'exp', 'seq'), scatter_dimension=0,...  642 us
    unnamed x13, waiting for transfers between devices  144 us
    unnamed x2, blocking collectives  134 us
    reduce_scatter x1, waiting for transfers between devices, local(): lax.psum_scatter(key_terms.reshape(length, 2 * KV * HD).astype(jnp.bfloat...  127 us
    all_gather x1, blocking collectives, local(): lax.all_gather(dense_shards[5], ('rep', 'exp', 'seq'), axis=0, tiled=True)  84.3 us
    reduce_scatter x1, waiting for transfers between devices, local(): lax.psum_scatter(grad_out_local.astype(jnp.bfloat16), ('rep', 'seq'), sca...  79.2 us
  transfers between devices with their start and end apart: 16, of which 14 were waited for; matrix products, arithmetic and copies ran while one was open for 5% of the time, Pallas kernels for 0%

commit v1 on v0

v1 whole, which is shorter than its diff:
```python
import functools

import jax
import jax.numpy as jnp
from jax import lax
from jax.experimental import pallas as pl
from jax.experimental.pallas import tpu as pltpu
from jax.sharding import PartitionSpec as P

H = 16
KV = 8
HD = 64
F = 512
TOP = 8
CAP = 64

epsilon = 1e-06
f32 = jnp.float32
bf16 = jnp.bfloat16

VMEM = pl.BlockSpec(memory_space=pltpu.VMEM)
SMEM = pl.BlockSpec(memory_space=pltpu.SMEM)


def dot(a, b):
    return jnp.dot(a, b, preferred_element_type=f32)


def dot_t(a, b):
    return lax.dot_general(a, b, (((1,), (1,)), ((), ())), preferred_element_type=f32)


def t_dot(a, b):
    return lax.dot_general(a, b, (((0,), (0,)), ((), ())), preferred_element_type=f32)


def call(body, out_shape, flops, nbytes, **kw):
    return pl.pallas_call(
        body,
        out_shape=out_shape,
        cost_estimate=pl.CostEstimate(flops=flops, bytes_accessed=nbytes, transcendentals=0),
        compiler_params=pltpu.CompilerParams(vmem_limit_bytes=60 * 1024 * 1024),
        **kw,
    )


def whole(body, out_shape, n_in, flops, nbytes, scalars=0, scratch=()):
    outs = jax.tree.map(lambda _: VMEM, out_shape)
    return call(
        body,
        out_shape,
        flops,
        nbytes,
        in_specs=[SMEM] * scalars + [VMEM] * (n_in - scalars),
        out_specs=outs,
        scratch_shapes=list(scratch),
    )


def shape(dims, dtype):
    return jax.ShapeDtypeStruct(dims, dtype)


def turn(vectors, cosine, sine):
    half = vectors.shape[0] // 2
    a, b = vectors[:half], vectors[half:]
    return jnp.concatenate([a * cosine - b * sine, b * cosine + a * sine], axis=0)


def lanes(rows):
    return lax.broadcasted_iota(jnp.int32, (rows, 128), 1)


def pack_kernel(
    q_ref, kv_ref, gain_ref, routes_ref, out_w_ref, router_ref, gain_two_ref, out_ref, rest_ref
):
    n, rows, _ = out_ref.shape
    width = out_w_ref.shape[1]
    experts = router_ref.shape[1]
    low = lanes(rows) < HD
    same = lax.broadcasted_iota(jnp.int32, (rows, rows), 0) == lax.broadcasted_iota(
        jnp.int32, (rows, rows), 1
    )

    def column(ref):
        return jnp.sum(jnp.where(same, ref[...].astype(f32), 0.0), axis=1, keepdims=True)

    gain = column(gain_ref)
    routes = routes_ref[...].astype(f32).astype(bf16)
    for e in range(n):
        at = e // 2 * 128
        key = kv_ref[:, at : at + 128].astype(f32)
        value = kv_ref[:, KV * HD + at : KV * HD + at + 128].astype(f32)
        if e % 2 == 0:
            pair = jnp.where(low, key, pltpu.roll(value, HD, 1))
        else:
            pair = jnp.where(low, pltpu.roll(key, HD, 1), value)
        query = q_ref[:, e * 2 * HD : (e + 1) * 2 * HD].astype(f32)
        out_ref[e] = jnp.concatenate(
            [(gain * query).astype(bf16), (gain * pair).astype(bf16), routes], axis=1
        )
    router = jnp.concatenate(
        [router_ref[...].astype(f32), jnp.zeros((rows, 128 - experts), f32)], axis=1
    )
    router = jnp.where(lanes(rows) == experts, column(gain_two_ref), router)
    rest_ref[...] = jnp.concatenate([out_w_ref[...], router.astype(bf16)], axis=1)


def pack_call(w_query, w_keyval, gain, routes, w_output, w_router, gain_two, n_exp):
    rows, width = w_output.shape
    return whole(
        pack_kernel,
        [shape((n_exp, rows, 4 * HD + 128), bf16), shape((rows, width + 128), bf16)],
        7,
        1000,
        n_exp * rows * 768,
    )(w_query, w_keyval, gain, routes, w_output, w_router, gain_two)


def group_sums(got_ref, n_exp, n_seq):
    n_all = got_ref.shape[0]
    total = []
    for e in range(n_exp):
        one = jnp.zeros(got_ref.shape[1:], f32)
        for r in range(n_all // (n_exp * n_seq)):
            for z in range(n_seq):
                one = one + got_ref[(r * n_exp + e) * n_seq + z].astype(f32)
        total.append(one)
    return total


def unpack_kernel(
    n_exp,
    n_seq,
    got_ref,
    wq_ref,
    wkv_ref,
    gain_ref,
    q_ref,
    kv_ref,
    out_ref,
    router_ref,
    gain_one_ref,
    gain_two_ref,
):
    total = group_sums(got_ref, n_exp, n_seq)
    rows = q_ref.shape[0]
    low = lanes(rows) < HD
    same = lax.broadcasted_iota(jnp.int32, (rows, rows), 0) == lax.broadcasted_iota(
        jnp.int32, (rows, rows), 1
    )
    gain = jnp.sum(jnp.where(same, gain_ref[...].astype(f32), 0.0), axis=1, keepdims=True)
    part = jnp.zeros((rows, 128), f32)
    for e in range(n_exp):
        at = slice(e * 2 * HD, (e + 1) * 2 * HD)
        part = part + wq_ref[:, at].astype(f32) * total[e][:, : 2 * HD]
        q_ref[:, at] = gain * total[e][:, : 2 * HD]
        out_ref[:, at] = total[e][:, 2 * HD : 4 * HD]
    for e in range(0, n_exp, 2):
        a = total[e][:, 4 * HD + 128 :]
        b = total[e + 1][:, 4 * HD + 128 :]
        at = e // 2 * 128
        for at, piece in (
            (at, jnp.where(low, a, pltpu.roll(b, HD, 1))),
            (at + KV * HD, jnp.where(low, pltpu.roll(a, HD, 1), b)),
        ):
            part = part + wkv_ref[:, at : at + 128].astype(f32) * piece
            kv_ref[:, at : at + 128] = gain * piece
    small = sum(one[:, 4 * HD : 4 * HD + 128] for one in total)
    experts = router_ref.shape[1]
    router_ref[...] = small[:, :experts]
    small = jnp.where(
        lanes(rows) == experts, jnp.sum(part, axis=1, keepdims=True), small
    )
    small = jnp.concatenate([small, jnp.zeros((128 - rows, 128), f32)], axis=0).T
    gain_one_ref[...] = small[experts : experts + 1, :rows]
    gain_two_ref[...] = small[experts + 1 : experts + 2, :rows]


def unpack_call(got, w_query, w_keyval, gain, experts, n_exp, n_seq):
    n_all, rows, _ = got.shape
    wide = shape((rows, H * HD), f32)
    one = shape((1, rows), f32)
    return whole(
        functools.partial(unpack_kernel, n_exp, n_seq),
        [wide, wide, wide, shape((rows, experts), f32), one, one],
        4,
        1000,
        n_all * rows * 1024,
    )(got, w_query, w_keyval, gain)


def qkv_kernel(*refs):
    n = len(refs) - 7
    toks = refs[:n]
    w_ref, cos_ref, sin_ref, q_ref, qt_ref, kv_ref, hidden = refs[n:]
    rows = toks[0].shape[0]
    for j in range(n):
        x = toks[j][...].astype(f32)
        inverse = lax.rsqrt(jnp.mean(x * x, axis=-1, keepdims=True) + epsilon)
        hidden[j * rows : (j + 1) * rows] = (x * inverse).astype(bf16)
    whole_raw = dot(hidden[...], w_ref[...])
    for j in range(n):
        raw = whole_raw[j * rows : (j + 1) * rows]
        cosine, sine = cos_ref[j], sin_ref[j]
        up = raw[:, : 2 * HD].T
        up = jnp.concatenate(
            [turn(up[:HD], cosine, sine), turn(up[HD:], cosine, sine)], axis=0
        ) * (HD**-0.5)
        qt_ref[j] = up.astype(bf16)
        q_ref[j] = up.T.astype(bf16)
        up = raw[:, 2 * HD :].T
        up = jnp.concatenate([turn(up[:HD], cosine, sine), up[HD:]], axis=0)
        kv_ref[j] = up.T.astype(bf16)


def qkv_call(toks, w, cosine, sine):
    n = len(toks)
    rows, width = toks[0].shape
    o = shape((n, rows, 2 * HD), bf16)
    return whole(
        qkv_kernel,
        [o, o, o],
        n + 3,
        2 * n * rows * width * 4 * HD,
        4 * n * rows * width,
        scratch=[pltpu.VMEM((n * rows, width), bf16)],
    )(*toks, w, cosine, sine)


def chip_of(h, own):
    n_x = 4
    return 2 * lax.rem(h + n_x - own[0], n_x)


def fill_keys(kvs, keys, keys_up, mask, own, rows):
    n_seq, n = len(kvs), kvs[0].shape[0]
    for j in range(n):
        for d in range(n_seq):
            piece = kvs[d][j]
            keys[j, d * rows : (d + 1) * rows] = piece
            keys_up[j, :, d * rows : (d + 1) * rows] = piece.T
    query = own[2] * rows + lax.rem(
        lax.broadcasted_iota(jnp.int32, (rows, 2 * rows), 1), jnp.int32(rows)
    )
    for d in range(n_seq):
        key = lax.rem(own[2] + d, n_seq) * rows + lax.broadcasted_iota(
            jnp.int32, (rows, 2 * rows), 0
        )
        mask[d * rows : (d + 1) * rows] = jnp.where(key <= query, 0.0, -1e30).astype(f32)


def side(x):
    return jnp.concatenate([x[:HD], x[HD:]], axis=1)


def stack(x):
    rows = x.shape[1] // 2
    return jnp.concatenate([x[:, :rows], x[:, rows:]], axis=0)


def attend_kernel(own, qt_ref, *refs):
    kvs = refs[:4]
    att_ref, up_ref, log_ref, keys, keys_up, mask = refs[4:]
    n, _, rows = qt_ref.shape
    own = [own[0], own[1], own[2]]
    fill_keys(kvs, keys, keys_up, mask, own, rows)

    wide = 4 * rows

    def pair(h, _):
        at = chip_of(h, own)
        early, late = at + own[1], at + 1 - own[1]
        query = jnp.concatenate([side(qt_ref[early]), side(qt_ref[late])], axis=1)
        query = jnp.concatenate([query, jnp.zeros_like(query)], axis=0)

        def step(state, blocks):
            top, total, acc = state
            new_top = top
            for _, scores in blocks:
                new_top = jnp.maximum(new_top, jnp.max(scores, axis=0, keepdims=True))
            shrink = jnp.exp(top - new_top)
            total = total * shrink
            acc = acc * shrink
            for i, scores in blocks:
                p = jnp.exp(scores - new_top)
                total = total + jnp.sum(p, axis=0, keepdims=True)
                acc = acc + dot(keys_up[i, HD:], p.astype(bf16))
            return new_top, total, acc

        def chunk(c, state):
            i = chip_of(c, own)
            return step(state, [(i, dot(keys[i], query)), (i + 1, dot(keys[i + 1], query))])

        state = (
            jnp.full((1, wide), -1e30, f32),
            jnp.zeros((1, wide), f32),
            jnp.zeros((HD, wide), f32),
        )
        state = lax.fori_loop(0, h, chunk, state)
        scores = dot(keys[early], query)
        last = dot(keys[late], query[:, 2 * rows :])
        first = step([v[:, : 2 * rows] for v in state], [(early, scores[:, : 2 * rows] + mask[...])])
        second = step(
            [v[:, 2 * rows :] for v in state],
            [(early, scores[:, 2 * rows :]), (late, last + mask[...])],
        )
        for j, (top, total, acc) in ((early, first), (late, second)):
            up = acc / total
            up_ref[j] = up
            log_ref[j] = top + jnp.log(total)
            att_ref[j] = stack(up).T.astype(bf16)
        return 0

    lax.fori_loop(0, n // 2, pair, 0)


def attend_call(own, qt, kvs):
    n, _, rows = qt.shape
    n_seq = len(kvs)
    return whole(
        attend_kernel,
        [
            shape((n, rows, 2 * HD), bf16),
            shape((n, HD, 2 * rows), f32),
            shape((n, 1, 2 * rows), f32),
        ],
        2 + n_seq,
        36 * 4 * 512 * 256 * 128 * 2,
        4 * n * rows * 2 * HD * (n_seq + 4),
        scalars=1,
        scratch=[
            pltpu.VMEM((n, n_seq * rows, 2 * HD), bf16),
            pltpu.VMEM((n, 2 * HD, n_seq * rows), bf16),
            pltpu.VMEM((n_seq * rows, 2 * rows), f32),
        ],
    )(own, qt, *kvs)


def attend_back_kernel(own, q_ref, qt_ref, up_ref, log_ref, got_ref, cos_ref, sin_ref, *refs):
    n, _, rows = qt_ref.shape
    kvs = refs[:4]
    dq_ref = refs[4]
    dkv_refs = refs[5:9]
    keys, keys_up, mask, grads_up, dkv = refs[9:]
    own = [own[0], own[1], own[2]]
    fill_keys(kvs, keys, keys_up, mask, own, rows)
    for j in range(n):
        grads_up[j] = got_ref[j, :, : 2 * HD].T
        dkv[j] = jnp.zeros(dkv.shape[1:], f32)
    low_lane = lanes(rows) < HD
    half = 2 * rows

    def pair(h, _):
        at = chip_of(h, own)
        early, late = at + own[1], at + 1 - own[1]
        query = jnp.concatenate([side(qt_ref[early]), side(qt_ref[late])], axis=1)
        grad = jnp.concatenate([side(grads_up[2 * h]), side(grads_up[2 * h + 1])], axis=1)
        up = jnp.concatenate([up_ref[early], up_ref[late]], axis=1)
        log_total = jnp.concatenate([log_ref[early], log_ref[late]], axis=1)
        delta = jnp.sum(up * grad.astype(f32), axis=0, keepdims=True)
        query = jnp.concatenate([query, jnp.zeros_like(query)], axis=0)
        grad = jnp.concatenate([jnp.zeros_like(grad), grad], axis=0)
        below_q, below_g = [], []
        for b, j in ((2 * h, early), (2 * h + 1, late)):
            q = q_ref[j].astype(f32)
            g = got_ref[b][:, : 2 * HD].astype(f32)
            below_q.append(
                jnp.concatenate(
                    [jnp.where(low_lane, q, 0.0), jnp.where(low_lane, pltpu.roll(q, HD, 1), 0.0)],
                    axis=0,
                ).astype(bf16)
            )
            below_g.append(
                jnp.concatenate(
                    [jnp.where(low_lane, 0.0, pltpu.roll(g, HD, 1)), jnp.where(low_lane, 0.0, g)],
                    axis=0,
                ).astype(bf16)
            )
        below = jnp.concatenate(below_q + below_g, axis=0)
        below_late = jnp.concatenate([below_q[1], below_g[1]], axis=0)

        def chunk(i, acc, scores, grad_p, log_, delta_, below_):
            p = jnp.exp(scores - log_)
            ds = (p * (grad_p - delta_)).astype(bf16)
            dkv[i] = dkv[i] + dot(jnp.concatenate([ds, p.astype(bf16)], axis=1), below_)
            return acc + dot(keys_up[i, :HD], ds)

        def full(c, acc):
            i = chip_of(c, own)
            for k in (i, i + 1):
                acc = chunk(
                    k, acc, dot(keys[k], query), dot(keys[k], grad), log_total, delta, below
                )
            return acc

        acc = lax.fori_loop(0, h, full, jnp.zeros((HD, 2 * half), f32))
        scores = dot(keys[early], query)
        scores = jnp.concatenate([scores[:, :half] + mask[...], scores[:, half:]], axis=1)
        acc = chunk(early, acc, scores, dot(keys[early], grad), log_total, delta, below)
        scores = dot(keys[late], query[:, half:]) + mask[...]
        last = chunk(
            late,
            acc[:, half:],
            scores,
            dot(keys[late], grad[:, half:]),
            log_total[:, half:],
            delta[:, half:],
            below_late,
        )
        for b, j, part in ((2 * h, early, acc[:, :half]), (2 * h + 1, late, last)):
            cosine, sine = cos_ref[j], -sin_ref[j]
            cosine = jnp.concatenate([cosine, cosine], axis=1)
            sine = jnp.concatenate([sine, sine], axis=1)
            dq_ref[b] = stack(turn(part * (HD**-0.5), cosine, sine)).T.astype(bf16)
        return 0

    lax.fori_loop(0, n // 2, pair, 0)
    for d, ref in enumerate(dkv_refs):
        for j in range(n):
            ref[j] = dkv[j, d * rows : (d + 1) * rows].astype(bf16)


def attend_back_call(own, q, qt, up, log_total, got, cosine, sine, kvs):
    n, _, rows = qt.shape
    n_seq = len(kvs)
    o = shape((n, rows, 2 * HD), bf16)
    return whole(
        attend_back_kernel,
        [o] * (1 + n_seq),
        8 + n_seq,
        36 * 10 * 512 * 256 * 128 * 2,
        4 * n * rows * 2 * HD * 10,
        scalars=1,
        scratch=[
            pltpu.VMEM((n, n_seq * rows, 2 * HD), bf16),
            pltpu.VMEM((n, 2 * HD, n_seq * rows), bf16),
            pltpu.VMEM((n_seq * rows, 2 * rows), f32),
            pltpu.VMEM((n, 2 * HD, rows), bf16),
            pltpu.VMEM((n, n_seq * rows, 2 * HD), f32),
        ],
    )(own, q, qt, up, log_total, got, cosine, sine, *kvs)


def early_kernel(n, order, left_ref, dq_ref, got_ref, router_grad, gain_two_grad, *refs):
    toks = refs[:n]
    out_ref, hidden, columns = refs[n:]
    rows, width = toks[0].shape
    for j in range(n):
        own = slice(j * rows, (j + 1) * rows)
        columns[: 2 * HD, own] = dq_ref[order[j]].T
        columns[2 * HD :, own] = got_ref[order[j]][:, 2 * HD :].T
        x = toks[j][...].astype(f32)
        x = x * lax.rsqrt(jnp.mean(x * x, axis=-1, keepdims=True) + epsilon)
        hidden[own] = x.astype(bf16)
    out_ref[:, : 2 * HD] = dot(columns[: 2 * HD], hidden[...]).T.astype(bf16)
    out_ref[:, 2 * HD : 4 * HD] = dot(columns[2 * HD :], left_ref[...]).T.astype(bf16)
    gains = jnp.concatenate(
        [jnp.zeros((33, width), f32), gain_two_grad[...], jnp.zeros((94, width), f32)], axis=0
    )
    out_ref[:, 4 * HD :] = (router_grad[...] + gains.T).astype(bf16)


def early_call(order, left, dq, got, router_grad, gain_two_grad, toks):
    n = len(toks)
    rows, width = toks[0].shape
    return whole(
        functools.partial(early_kernel, n),
        [shape((width, 4 * HD + 128), bf16), shape((n * rows, width), bf16)],
        6 + n,
        4 * n * rows * width * 128,
        n * rows * width * 6,
        scalars=1,
        scratch=[pltpu.VMEM((4 * HD, n * rows), bf16)],
    )(order, left, dq, got, router_grad, gain_two_grad, *toks)


def middle_kernel(n, own, order, w_ref, routes_ref, *refs):
    att = refs[:n]
    toks = refs[n : 2 * n]
    hid_ref, mid_ref, gates_ref, rank_ref, gate_up_ref, left, gain_ref, middles = refs[2 * n :]
    rows, width = toks[0].shape
    experts = rank_ref.shape[1]
    router = w_ref[:, width:]
    gain_ref[...] = router.astype(f32).T[experts : experts + 8]
    lane = lanes(rows)
    before = (
        lax.broadcasted_iota(jnp.int32, (rows, rows), 0)
        >= lax.broadcasted_iota(jnp.int32, (rows, rows), 1)
    ).astype(bf16)
    for k in range(n):
        column = pl.ds(pl.multiple_of(order[k] * 128, 128), 128)
        for j in range(n):
            source = 2 * ((j // 2 - k // 2) % (n // 2)) + ((j % 2) ^ (k % 2))
            left[j * rows : (j + 1) * rows, column] = att[k][source]
    middles[...] = dot(left[...], w_ref[:, :width])
    for j in range(n):
        middle = toks[j][...].astype(f32) + middles[j * rows : (j + 1) * rows]
        if j == 0:
            mid_ref[...] = middle
        inverse = lax.rsqrt(jnp.mean(middle * middle, axis=-1, keepdims=True) + epsilon)
        hid_ref[j] = (middle * inverse * gain_ref[0:1]).astype(bf16)
    for j in range(n):
        logits = dot(hid_ref[j], router)
        chosen = routes_ref[order[j]][:, 4 * HD :].astype(f32)
        chosen = jnp.concatenate([chosen, jnp.zeros((rows - TOP, rows), f32)], axis=0).T
        chosen = chosen.astype(jnp.int32)
        named = lane == chosen[:, 0:1]
        for k in range(1, TOP):
            named = jnp.logical_or(named, lane == chosen[:, k : k + 1])
        masked = jnp.where(named, logits, -1e30)
        top = jnp.max(masked, axis=-1, keepdims=True)
        e = jnp.where(named, jnp.exp(masked - top), 0.0)
        gates = e / jnp.sum(e, axis=-1, keepdims=True)
        if j == 0:
            gates_ref[...] = gates
        count = dot(before, named.astype(f32).astype(bf16))
        rank = jnp.where(named, count - 1.0, -1.0)
        rank_ref[j] = rank.T[:experts]
        gate_up_ref[j] = gates.T[:experts]


def middle_call(own, order, w, routes, att, toks, experts):
    n = len(att)
    rows, width = toks[0].shape
    return call(
        functools.partial(middle_kernel, n),
        [
            shape((n, rows, width), bf16),
            shape((rows, width), f32),
            shape((rows, 128), f32),
            shape((n, experts, rows), f32),
            shape((n, experts, rows), f32),
            shape((n * rows, width), bf16),
            shape((8, width), f32),
        ],
        2 * n * rows * width * (width + 128),
        2 * n * rows * width * 4,
        in_specs=[SMEM] * 2 + [VMEM] * (2 + 2 * n),
        out_specs=[VMEM] * 7,
        scratch_shapes=[pltpu.VMEM((n * rows, width), f32)],
    )(own, order, w, routes, *att, *toks)


def expert_kernel(
    first,
    hid_ref,
    cot_ref,
    swapped_ref,
    rank_ref,
    gate_ref,
    in_ref,
    out_ref,
    grad_ref,
    mix_keep,
    mix_swap,
    back_keep,
    back_swap,
    picks,
    xs,
    cots,
    gxs,
    mixes,
    backs,
    act_ref,
    gp_ref,
):
    e = pl.program_id(0)
    n, rows, width = hid_ref.shape
    here = xs.shape[0]
    slots = n * CAP
    experts = rank_ref.shape[1]

    @pl.when(e == 0)
    def _():
        slot = lax.broadcasted_iota(jnp.int32, (CAP, rows), 0).astype(f32)

        def gather(i, _):
            for b, source in ((2 * i, cot_ref), (2 * i + 1, swapped_ref)):
                own = pl.ds(pl.multiple_of(b * CAP, CAP), CAP)
                hots = [
                    (slot == rank_ref[b, pl.ds(first[0] + k, 1), :]).astype(f32)
                    for k in range(here)
                ]
                hot = jnp.concatenate(hots, axis=0)
                picks[b] = hot.T.astype(bf16)
                low = hot.astype(bf16)
                x = dot(low, hid_ref[b]).astype(bf16)
                g = dot(low, source[i])
                for k in range(here):
                    gate = jnp.sum(
                        hots[k] * gate_ref[b, pl.ds(first[0] + k, 1), :], axis=1, keepdims=True
                    )
                    part = slice(k * CAP, (k + 1) * CAP)
                    xs[k, own] = x[part]
                    cots[k, own] = g[part].astype(bf16)
                    gxs[k, own] = (gate * g[part]).astype(bf16)
                    mixes[k, own, :128] = jnp.broadcast_to(gate, (CAP, 128)).astype(f32)
            return 0

        lax.fori_loop(0, n // 2, gather, 0)

    w_in, w_out = in_ref[0], out_ref[0]
    half = slots // 2
    parts = [slice(0, half), slice(half, slots)]
    projected = [dot(xs[e, part], w_in) for part in parts]
    grad_active = [dot_t(gxs[e, part], w_out) for part in parts]
    lane = lax.broadcasted_iota(jnp.int32, (half, 128), 1)
    actives, gps = [], []
    for part, both, ga in zip(parts, projected, grad_active):
        gate_half = both[:, :F]
        up_half = both[:, F:]
        s = jax.nn.sigmoid(gate_half)
        silu = gate_half * s
        active = (silu * up_half).astype(bf16)
        gp = jnp.concatenate(
            [ga * up_half * s * (1.0 + gate_half * (1.0 - s)), ga * silu], axis=1
        ).astype(bf16)
        act_ref[part] = active
        gp_ref[part] = gp
        actives.append(active)
        gps.append(gp)
    for part, active, gp in zip(parts, actives, gps):
        produced = dot(active, w_out).astype(bf16).astype(f32)
        backs[e, part, :width] = dot_t(gp, w_in).astype(bf16)
        grad_gate = jnp.sum(cots[e, part].astype(f32) * produced, axis=-1, keepdims=True)
        high = grad_gate.astype(bf16).astype(f32)
        extra = jnp.where(lane == first[0] + e, high, 0.0) + jnp.where(
            lane == first[0] + e + experts, grad_gate - high, 0.0
        )
        backs[e, part, width:] = extra.astype(bf16)
        mixes[e, part] = mixes[e, part, :1] * produced
    n_out = grad_ref.shape[1]
    rows_in = width // n_out
    grad_ref[0, :, :rows_in] = t_dot(xs[e], gp_ref[...]).astype(bf16).reshape(n_out, rows_in, -1)
    grad_ref[0, :, rows_in:] = (
        t_dot(act_ref[...], gxs[e]).astype(bf16).reshape(n_out, F // n_out, -1)
    )

    @pl.when(e == here - 1)
    def _():

        def combine(i, _):
            for c, mix_ref, back_ref in ((0, mix_keep, back_keep), (1, mix_swap, back_swap)):
                b = 2 * i + c
                own = pl.ds(pl.multiple_of(b * CAP, CAP), CAP)
                pick = picks[b]
                mix = dot(
                    pick,
                    jnp.concatenate([mixes[k, own].astype(bf16) for k in range(here)], axis=0),
                )
                back = dot(pick, jnp.concatenate([backs[k, own] for k in range(here)], axis=0))
                mix_ref[i] = mix.astype(bf16)
                back_ref[i] = back.astype(bf16)
            return 0

        lax.fori_loop(0, n // 2, combine, 0)


def expert_call(first, hidden, cots, swapped, rank, gate, w_in, w_out, n_out):
    n, rows, width = hidden.shape
    here = w_in.shape[0]
    slots = n * CAP
    per = lambda *dims: pl.BlockSpec((1,) + dims, lambda e: (e, 0, 0))
    mix = shape((n // 2, rows, width), bf16)
    back = shape((n // 2, rows, width + 128), bf16)
    return call(
        expert_kernel,
        [
            shape((here, n_out, (width + F) // n_out, width), bf16),
            mix,
            mix,
            back,
            back,
        ],
        here * slots * width * F * 2 * 9,
        here * width * F * 6 + here * slots * width * 8,
        grid=(here,),
        in_specs=[SMEM] + [VMEM] * 5 + [per(width, 2 * F), per(F, width)],
        out_specs=[pl.BlockSpec((1, n_out, (width + F) // n_out, width), lambda e: (e, 0, 0, 0))]
        + [VMEM] * 4,
        scratch_shapes=[
            pltpu.VMEM((n, rows, here * CAP), bf16),
            pltpu.VMEM((here, slots, width), bf16),
            pltpu.VMEM((here, slots, width), bf16),
            pltpu.VMEM((here, slots, width), bf16),
            pltpu.VMEM((here, slots, width), f32),
            pltpu.VMEM((here, slots, width + 128), bf16),
            pltpu.VMEM((slots, F), bf16),
            pltpu.VMEM((slots, 2 * F), bf16),
        ],
    )(first, hidden, cots, swapped, rank, gate, w_in, w_out)


def norm_back_kernel(
    cot_ref, mid_ref, gates_ref, hid_ref, gain_ref, w_ref, *refs
):
    parts = refs[:4]
    gm_ref, send_ref, small_ref, gain_out = refs[4:]
    rows, width = mid_ref.shape
    got = parts[0][...].astype(f32)
    for part in parts[1:]:
        got = got + part[...].astype(f32)
    experts = 32
    extra = got[:, width:]
    grad_gates = extra + pltpu.roll(extra, 128 - experts, 1)
    gates = gates_ref[...]
    weighted = gates * grad_gates
    logits = (weighted - gates * jnp.sum(weighted, axis=-1, keepdims=True)).astype(bf16)
    grad = got[:, :width] + dot_t(logits, w_ref[:, width:])
    small_ref[...] = t_dot(hid_ref[0], logits)
    middle = mid_ref[...]
    inverse = lax.rsqrt(jnp.mean(middle * middle, axis=-1, keepdims=True) + epsilon)
    gain_out[...] = jnp.sum(grad * middle * inverse, axis=0, keepdims=True)
    scaled = grad * gain_ref[0:1]
    grad_middle = (
        cot_ref[...].astype(f32)
        + inverse * scaled
        - middle * (inverse * inverse * inverse) * jnp.mean(scaled * middle, axis=-1, keepdims=True)
    )
    gm_ref[...] = grad_middle
    branch = grad_middle.astype(bf16)
    attended = dot_t(branch, w_ref[:, :width]).astype(bf16)
    for e in range(send_ref.shape[0]):
        at = slice(e * 128, (e + 1) * 128)
        send_ref[e, :, :128] = attended[:, at]
        send_ref[e, :, 128:] = branch[:, at]


def norm_back_call(cot, middle, gates, hidden, gain, w, parts):
    rows, width = middle.shape
    n = hidden.shape[0]
    return call(
        norm_back_kernel,
        [
            shape((rows, width), f32),
            shape((n, rows, 256), bf16),
            shape((width, 128), f32),
            shape((1, width), f32),
        ],
        2 * rows * width * (width + 256),
        rows * width * 24 + 2 * width * width,
        grid=(1,),
        in_specs=[
            VMEM,
            VMEM,
            VMEM,
            pl.BlockSpec((1, rows, width), lambda i: (0, 0, 0)),
            VMEM,
            VMEM,
        ]
        + [VMEM] * 4,
        out_specs=[VMEM] * 4,
    )(cot, middle, gates, hidden, gain, w, *parts)


def key_grad_kernel(order, cos_ref, sin_ref, dq_ref, *refs):
    dkv = refs[:4]
    send_ref, up_ref = refs[4:]
    n, rows, _ = dq_ref.shape
    for j in range(n):
        kv = dkv[0][j].astype(f32)
        for other in dkv[1:]:
            kv = kv + other[j].astype(f32)
        up = kv.T
        up = jnp.concatenate([turn(up[:HD], cos_ref[j], -sin_ref[j]), up[HD:]], axis=0)
        up_ref[:, j * rows : (j + 1) * rows] = up.astype(bf16)
        send_ref[order[j], :, 2 * HD :] = up.T.astype(bf16)
        send_ref[j, :, : 2 * HD] = dq_ref[j]


def key_grad_call(order, cosine, sine, dq, dkv):
    n, rows, _ = dq.shape
    return whole(
        key_grad_kernel,
        [shape((n, rows, 4 * HD), bf16), shape((2 * HD, n * rows), bf16)],
        8,
        n * rows * 4 * HD * 10,
        n * rows * 4 * HD * 8,
        scalars=1,
    )(order, cosine, sine, dq, *dkv)


def key_weight_kernel(up_ref, hidden_ref, early_ref, out_ref):
    out_ref[:, : 4 * HD + 128] = early_ref[...]
    out_ref[:, 4 * HD + 128 :] = dot(up_ref[...], hidden_ref[...]).T.astype(bf16)


def key_weight_call(up, hidden, early):
    width = hidden.shape[1]
    return whole(
        key_weight_kernel,
        shape((width, 4 * HD + 256), bf16),
        3,
        2 * up.shape[0] * up.shape[1] * width,
        2 * width * (width + 1024),
    )(up, hidden, early)


def token_grad_kernel(got_ref, w_ref, tok_ref, mid_ref, out_ref):
    scaled = dot_t(got_ref[0], w_ref[0])
    for e in range(1, got_ref.shape[0]):
        scaled = scaled + dot_t(got_ref[e], w_ref[e])
    x = tok_ref[...].astype(f32)
    inverse = lax.rsqrt(jnp.mean(x * x, axis=-1, keepdims=True) + epsilon)
    out_ref[...] = (
        mid_ref[...]
        + inverse * scaled
        - x * (inverse * inverse * inverse) * jnp.mean(scaled * x, axis=-1, keepdims=True)
    )


def token_grad_call(got, w, tokens, grad_middle):
    rows, width = tokens.shape
    return whole(
        token_grad_kernel,
        shape((rows, width), f32),
        4,
        1000,
        1000,
    )(got, w, tokens, grad_middle)


def send_exp(x, dx, dc):
    n_x = lax.axis_size("exp") // 2
    pairs = [
        (2 * i + c, 2 * ((i + dx) % n_x) + (c ^ dc)) for i in range(n_x) for c in range(2)
    ]
    return lax.ppermute(x, "exp", pairs)


def send_ring(x, axis, d):
    n = lax.axis_size(axis)
    return lax.ppermute(x, axis, [(i, (i + d) % n) for i in range(n)])


def far_first(n):
    return sorted(range(1, n), key=lambda d: -min(d, n - d))


def gather_x(x):
    n_x = lax.axis_size("exp") // 2
    got = {dx: send_exp(x, n_x - dx, 0) for dx in far_first(n_x)}
    return [x] + [got[dx] for dx in range(1, n_x)]


def gather_cores(blocks):
    return [piece for block in blocks for piece in (block, send_exp(block, 0, 1))]


def gather_exp(x):
    return gather_cores(gather_x(x))


def chip_sums(keep, swap):
    got = send_exp(swap, 0, 1)
    return [
        (keep[dx].astype(f32) + got[dx].astype(f32)).astype(bf16) for dx in range(keep.shape[0])
    ]


def scatter_x(chip):
    got = {dx: send_exp(chip[dx], dx, 0) for dx in far_first(len(chip))}
    return [chip[0]] + [got[dx] for dx in range(1, len(chip))]


def gather_ring(x, axis):
    n = lax.axis_size(axis)
    got = {d: send_ring(x, axis, n - d) for d in far_first(n)}
    return [x] + [got[d] for d in range(1, n)]


def local(
    tokens,
    norm1_gain,
    w_query,
    w_keyval,
    w_output,
    norm2_gain,
    w_router,
    expert_in,
    expert_out,
    routes,
    cotangent,
):
    rows, width = tokens.shape
    experts = w_router.shape[1]
    n_rep, n_exp, n_seq = (lax.axis_size("rep"), lax.axis_size("exp"), lax.axis_size("seq"))
    shard = width // (n_rep * n_exp * n_seq)
    own_rep = lax.axis_index("rep")
    own_exp = lax.axis_index("exp")
    own_seq = lax.axis_index("seq")
    qcols = H // n_exp * HD
    here = expert_in.shape[0]
    n_x = n_exp // 2
    own = jnp.stack([own_exp // 2, lax.rem(own_exp, 2), own_seq]).astype(jnp.int32)
    relative = jnp.arange(n_exp, dtype=jnp.int32)
    order = 2 * lax.rem(own[0] + relative // 2, n_x) + lax.rem(own[1] + relative, 2)
    first = (own_exp * here).astype(jnp.int32).reshape(1)

    everyone = ("rep", "exp", "seq")
    n_all = n_rep * n_exp * n_seq

    columns, output_rows = pack_call(
        w_query,
        w_keyval,
        norm1_gain.reshape(1, shard),
        routes.T,
        w_output,
        w_router,
        norm2_gain.reshape(1, shard),
        n_exp,
    )
    columns = lax.all_to_all(columns, "exp", split_axis=0, concat_axis=0, tiled=True)
    columns, tokens_later = lax.optimization_barrier((columns, tokens))
    tok_blocks = gather_x(tokens_later)
    routes_g = columns
    columns = lax.all_to_all(
        jnp.broadcast_to(columns[None, :, :, : 4 * HD], (n_rep * n_seq, n_exp, shard, 4 * HD)),
        ("rep", "seq"),
        split_axis=0,
        concat_axis=0,
        tiled=True,
    )
    own_columns = (
        columns.reshape(n_rep, n_seq, n_exp, shard, 4 * HD)
        .transpose(0, 2, 1, 3, 4)
        .reshape(width, 4 * HD)
    )
    toks = gather_cores(tok_blocks)
    output_all = lax.all_gather(output_rows, everyone, axis=0, tiled=True)
    positions = (order[:, None] * n_seq + own_seq) * rows + jnp.arange(rows, dtype=jnp.int32)
    frequencies = 10000.0 ** (-(jnp.arange(HD // 2, dtype=f32) * 2.0 / HD))
    angles = positions.astype(f32)[:, None, :] * frequencies[None, :, None]
    cosine, sine = jnp.cos(angles), jnp.sin(angles)

    q, q_up, kv = qkv_call(toks, own_columns, cosine, sine)
    kv, cot = lax.optimization_barrier((kv, cotangent))
    kvs, cots = lax.optimization_barrier((gather_ring(kv, "seq"), gather_x(cot)))
    attended, att_up, log_total = attend_call(own, q_up, kvs)
    attended, cots = lax.optimization_barrier((attended, jnp.stack(cots)))
    cots_swapped = send_exp(cots, 0, 1)
    attended, own_columns = lax.optimization_barrier((gather_exp(attended), own_columns))
    qkv_all = lax.all_gather(own_columns, "exp", axis=0)
    hidden2, middle, gates, rank, gate_up, left, gains = middle_call(
        own, order, output_all, routes_g, attended, toks, experts
    )
    expert_grads, mix_keep, mix_swap, back_keep, back_swap = expert_call(
        first,
        hidden2,
        cots,
        cots_swapped,
        rank,
        gate_up,
        expert_in,
        expert_out,
        n_rep * n_seq,
    )

    expert_grads = lax.psum_scatter(
        expert_grads.reshape(here, -1, width), ("rep", "seq"), scatter_dimension=1, tiled=True
    ).astype(f32)
    parts = scatter_x(chip_sums(back_keep, back_swap))
    rows_in = width // (n_rep * n_seq)
    grad_expert_in = expert_grads[:, :rows_in]
    grad_expert_out = expert_grads[:, rows_in:]
    grad_middle, send, grad_router, grad_gain_two = norm_back_call(
        cotangent, middle, gates, hidden2, gains, output_all, parts
    )
    send, mix_keep, mix_swap = lax.optimization_barrier((send, mix_keep, mix_swap))
    mix = chip_sums(mix_keep, mix_swap)
    got = lax.all_to_all(send, "exp", split_axis=0, concat_axis=0, tiled=True)
    mix = scatter_x(mix)
    dq, *dkv = attend_back_call(own, q, q_up, att_up, log_total, got, cosine, sine, kvs)
    dkv, mix = lax.optimization_barrier((dkv, mix))
    output = (middle + sum(piece.astype(f32) for piece in mix)).astype(bf16)
    sent = {d: send_ring(dkv[d], "seq", d) for d in far_first(n_seq)}
    dkv = [dkv[0]] + [sent[d] for d in range(1, n_seq)]
    dkv[1], dq = lax.optimization_barrier((dkv[1], dq))
    early, hidden1 = early_call(order, left, dq, got, grad_router, grad_gain_two, toks)
    dq, early = lax.optimization_barrier((dq, early))
    send, dkv_up = key_grad_call(order, cosine, sine, dq, dkv)
    got = lax.all_to_all(send, "exp", split_axis=0, concat_axis=0, tiled=True)
    dense = key_weight_call(dkv_up, hidden1, early)
    got, _ = lax.optimization_barrier((got, dense))
    dense = lax.all_to_all(
        dense.reshape(n_all, shard, -1), everyone, split_axis=0, concat_axis=0, tiled=True
    )
    grad_tokens = token_grad_call(got, qkv_all, tokens, grad_middle)
    dense, grad_tokens, grad_expert_in, grad_expert_out = lax.optimization_barrier(
        (dense, grad_tokens, grad_expert_in, grad_expert_out)
    )
    grad_query, grad_keyval, grad_output, grad_router, grad_gain_one, grad_gain_two = unpack_call(
        dense, w_query, w_keyval, norm1_gain.reshape(1, shard), experts, n_exp, n_seq
    )
    return (
        output,
        grad_tokens,
        grad_gain_one.reshape(shard),
        grad_query,
        grad_keyval,
        grad_output,
        grad_gain_two.reshape(shard),
        grad_router,
        grad_expert_in,
        grad_expert_out,
    )


def solution(mesh):
    placed = (
        P(("rep", "exp", "seq"), None),
        P(("rep", "exp", "seq")),
        P(("rep", "exp", "seq"), None),
        P(("rep", "exp", "seq"), None),
        P(("rep", "exp", "seq"), None),
        P(("rep", "exp", "seq")),
        P(("rep", "exp", "seq"), None),
        P("exp", None, None),
        P("exp", None, None),
        P(("rep", "exp", "seq"), None),
        P(("rep", "exp", "seq"), None),
    )
    return jax.shard_map(
        local,
        mesh=mesh,
        in_specs=placed,
        out_specs=(
            P(("rep", "exp", "seq"), None),
            P(("rep", "exp", "seq"), None),
            P(("rep", "exp", "seq")),
            P(("rep", "exp", "seq"), None),
            P(("rep", "exp", "seq"), None),
            P(("rep", "exp", "seq"), None),
            P(("rep", "exp", "seq")),
            P(("rep", "exp", "seq"), None),
            P("exp", ("rep", "seq"), None),
            P("exp", ("rep", "seq"), None),
        ),
        check_vma=False,
    )
```

time: 3100 us -> 274 us (0.09)
  waiting for transfers between devices: 2590 us -> 85.3 us
  blocking collectives: 218 us -> 0 us
  Pallas kernels: 0 us -> 101 us
  matrix products: 91.1 us -> 0 us
  local copies, waits for them, and re-layouts: 101 us -> 12.5 us
    reduce_scatter x6 -> x1, waiting for transfers between devices: 2150 us -> 0.01 us  [local(): lax.psum_scatter(expert_grads.reshape(here, -1, width), ('rep', 'seq'), s...]
    all_gather x5 -> x2, waiting for transfers between devices: 185 us -> 0.01 us  [the longest x1 0.01 us: local(): output_all = lax.all_gather(output_rows, everyone, axis=0, tiled=True)]
    unnamed x13 -> x3, waiting for transfers between devices: 144 us -> 0.05 us
    unnamed x2 -> x0, blocking collectives: 134 us -> none
    pallas_call x0 -> x12, Pallas kernels: none -> 101 us  [the longest x1 33 us: expert_call(): call(expert_kernel, [shape((here, n_out, (width + F) // n_out, width), bf...]
    dot_general x25 -> x0, matrix products: 91.1 us -> none  [the longest x1 12.4 us: local(): jnp.einsum('sjcd,jdf->sjcf', arrived, expert_in, preferred_element_type=f32)]
    all_gather x1 -> x0, blocking collectives: 84.3 us -> none  [local(): lax.all_gather(dense_shards[5], ('rep', 'exp', 'seq'), axis=0, tiled=True)]
    all_to_all x4 -> x5, waiting for transfers between devices: 108 us -> 31.3 us  [the longest x2 10.5 us: local(): got = lax.all_to_all(send, 'exp', split_axis=0, concat_axis=0, tiled=True)]
  transfers between devices with their start and end apart: 16 -> 40, of which waited for: 14 -> 18; matrix products, arithmetic and copies ran while one was open for 5% -> 4% of each run, Pallas kernels for 0% -> 36%
where the time goes in v1:
time: 274 us; the launch traced here: 272 us
  Pallas kernels  101 us (37%)
  waiting for transfers between devices  85.3 us (31%)
  starting transfers between devices  54.3 us (20%)
  between operations  14.1 us (5%)
  local copies, waits for them, and re-layouts  12.5 us (5%)
  other arithmetic  5.67 us (2%)
    ppermute x26, waiting for transfers between devices, send_exp(): return lax.ppermute(x, 'exp', pairs)  36.4 us
    pallas_call x1, Pallas kernels, expert_call(): call(expert_kernel, [shape((here, n_out, (width + F) // n_out, width), bf...  33 us
    ppermute x26, starting transfers between devices, send_exp(): return lax.ppermute(x, 'exp', pairs)  19 us
    ppermute x6, waiting for transfers between devices, send_ring(): return lax.ppermute(x, axis, [(i, (i + d) % n) for i in range(n)])  17.5 us
    pallas_call x1, Pallas kernels, attend_back_call(): whole(attend_back_kernel, [o] * (1 + n_seq), 8 + n_seq, 36 * 10 * 512 * 2...  17 us
    pallas_call x1, Pallas kernels, attend_call(): whole(attend_kernel, [shape((n, rows, 2 * HD), bf16), shape((n, HD, 2 * r...  13.6 us
    all_to_all x2, waiting for transfers between devices, local(): got = lax.all_to_all(send, 'exp', split_axis=0, concat_axis=0, tiled=True)  10.5 us
    all_to_all x1, waiting for transfers between devices, local(): lax.all_to_all(dense.reshape(n_all, shard, -1), everyone, split_axis=0, c...  9.88 us
  transfers between devices with their start and end apart: 40, of which 18 were waited for; matrix products, arithmetic and copies ran while one was open for 4% of the time, Pallas kernels for 36%

profile of v1, /device:TPU:0, one launch (start us, length us, event | category | flops | bytes accessed | tf_op | source)
XLA Modules:
  0.0 272.4 jit_solution(12144053027310547412)
XLA Ops:
  7.2 1.5 shard_map.186
  8.8 4.4 %all-to-all-start = ((bf16[8,8,384]{2,1,0:T(8,128)(2,1)}), bf16[8,8,384]{2,1,0:T(8,128)(2,1)S(1)}, u32[]{:S(2)}, u32[]{:S(2)}) async-start(bf16[8,8,384]{2,1,0:T(8,128)(2,1)} %get-tuple-element.93), calls=%async_computation | async-start | bytes 98304 | tf_op jit(solution)/shard_map/all_to_all | solution.py:914
  13.2 5.5 %all-to-all-done.routes_ref = bf16[8,8,384]{2,1,0:T(8,128)(2,1)S(1)} async-done(((bf16[8,8,384]{2,1,0:T(8,128)(2,1)}), bf16[8,8,384]{2,1,0:T(8,128)(2,1)S(1)}, u32[]{:S(2)}, u32[]{:S(2)}) %all-to-all-start) | async-done | bytes 49184 | tf_op jit(solution)/shard_map/all_to_all | solution.py:914
  18.7 1.2 collective-permute-start.1
  19.9 1.5 collective-permute-start.3
  21.9 0.8 broadcast_in_dim.2
  22.7 8.0 %all-to-all-start.1 = ((bf16[16,8,8,256]{3,2,1,0:T(8,128)(2,1)}), bf16[16,8,8,256]{3,2,1,0:T(8,128)(2,1)S(1)}, u32[]{:S(2)}, u32[]{:S(2)}) async-start(bf16[16,8,8,256]{3,2,1,0:T(8,128)(2,1)} %broadcast_in_dim.2), calls=%async_computation.1 | async-start | bytes 1048576 | tf_op jit(solution)/shard_map/all_to_all | solution.py:918
  31.5 3.5 %collective-permute-done.5.refs_6_.refs_14_ = bf16[128,1024]{1,0:T(8,128)(2,1)S(1)} collective-permute-done((bf16[128,1024]{1,0:T(8,128)(2,1)}, bf16[128,1024]{1,0:T(8,128)(2,1)S(1)}, u32[]{:S(2)}, u32[]{:S(2)}) %collective-permute-start.5) | collective-permute-done | bytes 262176 | tf_op jit(solution)/shard_map/ppermute | solution.py:829
  35.1 1.2 multiply_sine_fusion
  36.3 5.4 %all-to-all-done.1 = bf16[16,8,8,256]{3,2,1,0:T(8,128)(2,1)S(1)} async-done(((bf16[16,8,8,256]{3,2,1,0:T(8,128)(2,1)}), bf16[16,8,8,256]{3,2,1,0:T(8,128)(2,1)S(1)}, u32[]{:S(2)}, u32[]{:S(2)}) %all-to-all-start.1) | async-done | bytes 524320 | tf_op jit(solution)/shard_map/all_to_all | solution.py:918
  41.7 0.9 copy.21
  42.7 0.6 copy-done.12
  43.5 4.0 %shard_map.187 = (bf16[8,128,128]{2,1,0:T(8,128)(2,1)}, bf16[8,128,128]{2,1,0:T(8,128)(2,1)}, bf16[8,128,128]{2,1,0:T(8,128)(2,1)}) custom-call(bf16[128,1024]{1,0:T(8,128)(2,1)} %tok_ref.1, bf16[128,1024]{1,0:T(8,128)(2,1)} %copy-done.12, bf16[128,1024]{1,0:T(8,128)(2,1)} %copy-done.9, bf16[128,1024]{1,0:T(8,128)(2,1)} %copy-done.13, ...), custom_call_target="tpu_custom_call" | custom-call | flops 536870912 | bytes 4194304 | tf_op jit(solution)/shard_map/pallas_call | solution.py:221
  48.1 2.1 collective-permute-start.8
  50.2 2.9 %collective-permute-start.10 = (bf16[128,1024]{1,0:T(8,128)(2,1)S(1)}, bf16[128,1024]{1,0:T(8,128)(2,1)S(1)}, u32[]{:S(2)}, u32[]{:S(2)}) collective-permute-start(bf16[128,1024]{1,0:T(8,128)(2,1)S(1)} %copy-done.8), channel_id=1, source_target_pairs={{0,24},{4,28},{8,0},{12,4},{16,8},{20,12},{24,16},{28,20},{1,25},{... | collective-permute-start | bytes 786440 | tf_op jit(solution)/shard_map/ppermute | solution.py:829
  53.1 0.8 collective-permute-start.11
  54.0 5.2 %collective-permute-done.7.refs_1_ = bf16[8,128,128]{2,1,0:T(8,128)(2,1)S(1)} collective-permute-done((bf16[8,128,128]{2,1,0:T(8,128)(2,1)}, bf16[8,128,128]{2,1,0:T(8,128)(2,1)S(1)}, u32[]{:S(2)}, u32[]{:S(2)}) %collective-permute-start.7) | collective-permute-done | bytes 262176 | tf_op jit(solution)/shard_map/ppermute | solution.py:834
  59.2 0.6 pad_add_fusion.own
  59.8 3.0 %collective-permute-done.9.refs_3_ = bf16[8,128,128]{2,1,0:T(8,128)(2,1)S(1)} collective-permute-done((bf16[8,128,128]{2,1,0:T(8,128)(2,1)}, bf16[8,128,128]{2,1,0:T(8,128)(2,1)S(1)}, u32[]{:S(2)}, u32[]{:S(2)}) %collective-permute-start.9) | collective-permute-done | bytes 262176 | tf_op jit(solution)/shard_map/ppermute | solution.py:834
  62.8 4.0 %collective-permute-done.12 = bf16[128,1024]{1,0:T(8,128)(2,1)S(1)} collective-permute-done((bf16[128,1024]{1,0:T(8,128)(2,1)S(1)}, bf16[128,1024]{1,0:T(8,128)(2,1)S(1)}, u32[]{:S(2)}, u32[]{:S(2)}) %collective-permute-start.12) | collective-permute-done | bytes 262176 | tf_op jit(solution)/shard_map/ppermute | solution.py:829
  66.9 13.6 %shard_map.188 = (bf16[8,128,128]{2,1,0:T(8,128)(2,1)}, f32[8,64,256]{2,1,0:T(8,128)}, f32[8,1,256]{2,1,0:T(1,128)}) custom-call(s32[3]{0:T(128)} %pad_add_fusion.own, bf16[8,128,128]{2,1,0:T(8,128)(2,1)} %get-tuple-element.96.qt_ref, bf16[8,128,128]{2,1,0:T(8,128)(2,1)} %get-tuple-element.100.refs_0_, bf16[8,128,128]{2,1,0:T(8,128)(2,1)} %copy-done.25, ...), custom_call_target="tpu_custom_call" | custom-call | flops 4831838208 | bytes 4194304 | tf_op jit(solution)/shard_map/pallas_call | solution.py:321
  80.5 0.9 collective-permute-start.16
  81.4 1.1 collective-permute-start.18
  82.6 6.6 %collective-permute-done.14.refs_2_ = bf16[8,128,128]{2,1,0:T(8,128)(2,1)S(1)} collective-permute-done((bf16[8,128,128]{2,1,0:T(8,128)(2,1)}, bf16[8,128,128]{2,1,0:T(8,128)(2,1)S(1)}, u32[]{:S(2)}, u32[]{:S(2)}) %collective-permute-start.14) | collective-permute-done | bytes 262176 | tf_op jit(solution)/shard_map/ppermute | solution.py:829
  89.2 1.4 collective-permute-done.16.refs_4_
  90.7 2.7 collective-permute-done.18.refs_6_
  93.4 1.5 collective-permute-done.19.refs_7_
  94.9 0.7 copy-done.34
  95.8 8.4 %shard_map.189 = (bf16[8,128,1024]{2,1,0:T(8,128)(2,1)}, f32[128,1024]{1,0:T(8,128)}, f32[128,128]{1,0:T(8,128)}, f32[8,32,128]{2,1,0:T(8,128)}, f32[8,32,128]{2...) custom-call(s32[3]{0:T(128)} %pad_add_fusion.own, s32[8]{0:T(128)} %get-tuple-element.175.order, ...), custom_call_target="tpu_custom_call" | custom-call | flops 2415919104 | bytes 8388608 | tf_op jit(solution)/shard_map/pallas_call | solution.py:526
  104.2 1.0 copy-done.24
  105.3 33.0 %shard_map.190 = (bf16[4,16,96,1024]{3,2,1,0:T(8,128)(2,1)}, bf16[4,128,1024]{2,1,0:T(8,128)(2,1)}, bf16[4,128,1024]{2,1,0:T(8,128)(2,1)}, bf16[4,128,1152]{2,1,0:T(8,128)(2,1)}, bf16[4,128,1152]{2,1,0:T(8,128)(2,1)}) custom-call(s32[1]{0:T(128)} %bitcast.13.first, bf16[8,128,1024]{2,1,0:T(8,128)(2,1)} %get-tuple-element.123.hid_ref, ...), custom_call_target="tpu_custom_call" | custom-call | flops 19327352832 | bytes 29360128 | tf_op jit(solution)/shard_map/pallas_call | solution.py:667
  138.3 1.2 copy-done.23
  140.0 2.5 collective-permute-done.21
  142.4 1.0 fusion.3
  143.5 2.9 %collective-permute-start.23 = (bf16[128,1152]{1,0:T(8,128)(2,1)S(1)}, bf16[128,1152]{1,0:T(8,128)(2,1)S(1)}, u32[]{:S(2)}, u32[]{:S(2)}) collective-permute-start(bf16[128,1152]{1,0:T(8,128)(2,1)S(1)} %get-tuple-element.177), channel_id=1, source_target_pairs={{0,16},{4,20},{8,24},{12,28},{16,0},{20,4},{24,8},{28,12},{1,17},{... | collective-permute-start | bytes 884744 | tf_op jit(solution)/shard_map/ppermute | solution.py:829
  146.7 13.6 %collective-permute-done.22.refs_1_ = bf16[128,1152]{1,0:T(8,128)(2,1)S(1)} collective-permute-done((bf16[128,1152]{1,0:T(8,128)(2,1)S(1)}, bf16[128,1152]{1,0:T(8,128)(2,1)S(1)}, u32[]{:S(2)}, u32[]{:S(2)}) %collective-permute-start.22) | collective-permute-done | bytes 294944 | tf_op jit(solution)/shard_map/ppermute | solution.py:829
  160.3 0.6 collective-permute-done.24.refs_3_
  161.6 4.8 %shard_map.191 = (f32[128,1024]{1,0:T(8,128)}, bf16[8,128,256]{2,1,0:T(8,128)(2,1)}, f32[1024,128]{1,0:T(8,128)}, f32[1,1024]{1,0:T(1,128)}) custom-call(bf16[128,1024]{1,0:T(8,128)(2,1)} %cot_ref.1, f32[128,1024]{1,0:T(8,128)} %get-tuple-element.118.mid_ref, f32[128,128]{1,0:T(8,128)} %get-tuple-element.122.gates_ref, ...), custom_call_target="tpu_custom_call" | custom-call | flops 335544320 | bytes 5242880 | tf_op jit(solution)/shard_map/pallas_call | solution.py:733
  166.4 3.7 %all-to-all-start.2 = ((bf16[8,128,256]{2,1,0:T(8,128)(2,1)}), bf16[8,128,256]{2,1,0:T(8,128)(2,1)S(1)}, u32[]{:S(2)}, u32[]{:S(2)}) async-start(bf16[8,128,256]{2,1,0:T(8,128)(2,1)} %get-tuple-element.133), calls=%async_computation.2 | async-start | bytes 1048576 | tf_op jit(solution)/shard_map/all_to_all | solution.py:972
  170.1 1.2 fusion.7
  171.3 2.0 collective-permute-start.26
  173.4 2.7 collective-permute-start.27
  176.0 1.5 collective-permute-start.28
  177.5 3.5 %all-to-all-done.2.got_ref = bf16[8,128,256]{2,1,0:T(8,128)(2,1)S(1)} async-done(((bf16[8,128,256]{2,1,0:T(8,128)(2,1)}), bf16[8,128,256]{2,1,0:T(8,128)(2,1)S(1)}, u32[]{:S(2)}, u32[]{:S(2)}) %all-to-all-start.2) | async-done | bytes 524320 | tf_op jit(solution)/shard_map/all_to_all | solution.py:972
  181.0 0.8 copy-done.3
  181.8 17.0 %shard_map.192 = (bf16[8,128,128]{2,1,0:T(8,128)(2,1)}, bf16[8,128,128]{2,1,0:T(8,128)(2,1)}, bf16[8,128,128]{2,1,0:T(8,128)(2,1)}, bf16[8,128,128]{2,1,0:T(8,128)(2,1)}, bf16[8,128,128]{2,1,0:T(8,128)(2,1)}) custom-call(s32[3]{0:T(128)} %pad_add_fusion.own, bf16[8,128,128]{2,1,0:T(8,128)(2,1)} %get-tuple-element.119.q_ref, ...), custom_call_target="tpu_custom_call" | custom-call | flops 12079595520 | bytes 5242880 | tf_op jit(solution)/shard_map/pallas_call | solution.py:428
  199.1 4.9 %collective-permute-start.30 = (bf16[8,128,128]{2,1,0:T(8,128)(2,1)}, bf16[8,128,128]{2,1,0:T(8,128)(2,1)S(1)}, u32[]{:S(2)}, u32[]{:S(2)}) collective-permute-start(bf16[8,128,128]{2,1,0:T(8,128)(2,1)} %get-tuple-element.154), channel_id=1, source_target_pairs={{0,2},{1,3},{2,0},{3,1},{4,6},{5,7},{6,4},{7,5},{8,10},{9,11},{10,... | collective-permute-start | bytes 786440 | tf_op jit(solution)/shard_map/ppermute | solution.py:834
  204.6 8.1 %collective-permute-done.29.refs_1_ = bf16[8,128,128]{2,1,0:T(8,128)(2,1)S(1)} collective-permute-done((bf16[8,128,128]{2,1,0:T(8,128)(2,1)}, bf16[8,128,128]{2,1,0:T(8,128)(2,1)S(1)}, u32[]{:S(2)}, u32[]{:S(2)}) %collective-permute-start.29) | collective-permute-done | bytes 262176 | tf_op jit(solution)/shard_map/ppermute | solution.py:834
  212.7 5.1 %shard_map.193 = (bf16[1024,384]{1,0:T(8,128)(2,1)}, bf16[1024,1024]{1,0:T(8,128)(2,1)}) custom-call(s32[8]{0:T(128)} %get-tuple-element.175.order, bf16[1024,1024]{1,0:T(8,128)(2,1)} %get-tuple-element.147.left_ref, bf16[8,128,128]{2,1,0:T(8,128)(2,1)} %get-tuple-element.151.dq_ref, bf16[8,128,256]{2,1,0:T(8,128)(2,1)} %copy-done.3, ...), custom_call_target="tpu_custom_call" | custom-call | flops 536870912 | bytes 6291456 | tf_op jit(solution)/shard_map/pallas_call | solution.py:467
  217.8 1.2 collective-permute-done.30.refs_2_
  219.0 0.7 copy-done.20
  219.7 0.7 copy-done.21
  220.4 2.7 shard_map.194
  223.1 4.2 %all-to-all-start.4 = ((bf16[8,128,256]{2,1,0:T(8,128)(2,1)}), bf16[8,128,256]{2,1,0:T(8,128)(2,1)S(1)}, u32[]{:S(2)}, u32[]{:S(2)}) async-start(bf16[8,128,256]{2,1,0:T(8,128)(2,1)} %get-tuple-element.159), calls=%async_computation.4 | async-start | bytes 1048576 | tf_op jit(solution)/shard_map/all_to_all | solution.py:983
  227.2 3.4 %shard_map.195 = bf16[1024,512]{1,0:T(8,128)(2,1)} custom-call(bf16[128,1024]{1,0:T(8,128)(2,1)} %get-tuple-element.156.up_ref, bf16[1024,1024]{1,0:T(8,128)(2,1)} %get-tuple-element.157.hidden_ref, bf16[1024,384]{1,0:T(8,128)(2,1)} %get-tuple-element.158.early_ref), custom_call_target="tpu_custom_call" | custom-call | flops 268435456 | bytes 4194304 | tf_op jit(solution)/shard_map/pallas_call | solution.py:791
  230.6 7.0 %all-to-all-done.4.got_ref = bf16[8,128,256]{2,1,0:T(8,128)(2,1)S(1)} async-done(((bf16[8,128,256]{2,1,0:T(8,128)(2,1)}), bf16[8,128,256]{2,1,0:T(8,128)(2,1)S(1)}, u32[]{:S(2)}, u32[]{:S(2)}) %all-to-all-start.4) | async-done | bytes 524320 | tf_op jit(solution)/shard_map/all_to_all | solution.py:983
  237.6 6.5 %all-to-all-start.3 = ((bf16[128,8,512]{2,1,0:T(8,128)(2,1)}), bf16[128,8,512]{2,1,0:T(8,128)(2,1)S(1)}, u32[]{:S(2)}, u32[]{:S(2)}) async-start(bf16[128,8,512]{2,1,0:T(8,128)(2,1)} %bitcast.40), calls=%async_computation.3 | async-start | bytes 2097152 | tf_op jit(solution)/shard_map/all_to_all | solution.py:986
  244.1 0.9 add_convert_fusion.4
  245.0 4.9 %shard_map.196 = f32[128,1024]{1,0:T(8,128)} custom-call(bf16[8,128,256]{2,1,0:T(8,128)(2,1)} %copy-done.4, bf16[8,1024,256]{2,1,0:T(8,128)(2,1)} %bitcast.39, bf16[128,1024]{1,0:T(8,128)(2,1)} %tok_ref.1, f32[128,1024]{1,0:T(8,128)} %get-tuple-element.162.mid_ref), custom_call_target="tpu_custom_call" | custom-call | flops 1000 | bytes 1000 | tf_op jit(solution)/shard_map/pallas_call | solution.py:815
  249.9 2.2 slice.84
  252.1 0.8 slice.85
  253.0 9.9 %all-to-all-done.3.got_ref = bf16[128,8,512]{2,1,0:T(8,128)(2,1)S(1)} async-done(((bf16[128,8,512]{2,1,0:T(8,128)(2,1)}), bf16[128,8,512]{2,1,0:T(8,128)(2,1)S(1)}, u32[]{:S(2)}, u32[]{:S(2)}) %all-to-all-start.3) | async-done | bytes 1048608 | tf_op jit(solution)/shard_map/all_to_all | solution.py:986
  262.9 1.0 copy-done
  263.8 2.1 shard_map.197
  (115 shorter events, 4.8 us)
Async XLA Ops:
  7.2 88.6 %all-gather.4.cloned.1.call-start = ((), (), s32[]{:S(2)}) async-start(), calls=%async_computation.6 | async-start | bytes 2377728 | tf_op jit(solution)/shard_map/all_gather | solution.py:931
  8.8 9.9 %all-to-all-start = ((bf16[8,8,384]{2,1,0:T(8,128)(2,1)}), bf16[8,8,384]{2,1,0:T(8,128)(2,1)S(1)}, u32[]{:S(2)}, u32[]{:S(2)}) async-start(bf16[8,8,384]{2,1,0:T(8,128)(2,1)} %get-tuple-element.93), calls=%async_computation | async-start | bytes 98304 | tf_op jit(solution)/shard_map/all_to_all | solution.py:914
  18.7 28.9 %copy-start.22 = (bf16[8,8,384]{2,1,0:T(8,128)(2,1)}, bf16[8,8,384]{2,1,0:T(8,128)(2,1)S(1)}, u32[]{:S(2)}) copy-start(bf16[8,8,384]{2,1,0:T(8,128)(2,1)S(1)} %all-to-all-done.routes_ref) | copy-start | bytes 147460
  18.7 12.2 %collective-permute-start.1 = (bf16[128,1024]{1,0:T(8,128)(2,1)}, bf16[128,1024]{1,0:T(8,128)(2,1)S(1)}, u32[]{:S(2)}, u32[]{:S(2)}) collective-permute-start(bf16[128,1024]{1,0:T(8,128)(2,1)} %tok_ref.1), channel_id=1, source_target_pairs={{0,24},{4,28},{8,0},{12,4},{16,8},{20,12},{24,16},{28,20},{1,25},{... | collective-permute-start | bytes 786440 | tf_op jit(solution)/shard_map/ppermute | solution.py:829
  19.9 11.6 %collective-permute-start.3 = (bf16[128,1024]{1,0:T(8,128)(2,1)}, bf16[128,1024]{1,0:T(8,128)(2,1)S(1)}, u32[]{:S(2)}, u32[]{:S(2)}) collective-permute-start(bf16[128,1024]{1,0:T(8,128)(2,1)} %tok_ref.1), channel_id=1, source_target_pairs={{0,16},{4,20},{8,24},{12,28},{16,0},{20,4},{24,8},{28,12},{1,17},{... | collective-permute-start | bytes 786440 | tf_op jit(solution)/shard_map/ppermute | solution.py:829
  21.3 13.7 %collective-permute-start.5 = (bf16[128,1024]{1,0:T(8,128)(2,1)}, bf16[128,1024]{1,0:T(8,128)(2,1)S(1)}, u32[]{:S(2)}, u32[]{:S(2)}) collective-permute-start(bf16[128,1024]{1,0:T(8,128)(2,1)} %tok_ref.1), channel_id=1, source_target_pairs={{0,8},{4,12},{8,16},{12,20},{16,24},{20,28},{24,0},{28,4},{1,9},{5... | collective-permute-start | bytes 786440 | tf_op jit(solution)/shard_map/ppermute | solution.py:829
  22.7 19.0 %all-to-all-start.1 = ((bf16[16,8,8,256]{3,2,1,0:T(8,128)(2,1)}), bf16[16,8,8,256]{3,2,1,0:T(8,128)(2,1)S(1)}, u32[]{:S(2)}, u32[]{:S(2)}) async-start(bf16[16,8,8,256]{3,2,1,0:T(8,128)(2,1)} %broadcast_in_dim.2), calls=%async_computation.1 | async-start | bytes 1048576 | tf_op jit(solution)/shard_map/all_to_all | solution.py:918
  30.8 214.3 %all-gather.6.cloned.1.call-start = ((), (), s32[]{:S(2)}) async-start(), calls=%async_computation.8 | async-start | bytes 4718592 | tf_op jit(solution)/shard_map/all_gather | solution.py:944
  30.9 11.7 %collective-permute-start = (bf16[128,1024]{1,0:T(8,128)(2,1)}, bf16[128,1024]{1,0:T(8,128)(2,1)S(1)}, u32[]{:S(2)}, u32[]{:S(2)}) collective-permute-start(bf16[128,1024]{1,0:T(8,128)(2,1)} %tok_ref.1), channel_id=1, source_target_pairs={{0,4},{4,0},{8,12},{12,8},{16,20},{20,16},{24,28},{28,24},{1,5},{5... | collective-permute-start | bytes 786440 | tf_op jit(solution)/shard_map/ppermute | solution.py:829
  30.9 11.7 %copy-start.9 = (bf16[128,1024]{1,0:T(8,128)(2,1)}, bf16[128,1024]{1,0:T(8,128)(2,1)S(1)}, u32[]{:S(2)}) copy-start(bf16[128,1024]{1,0:T(8,128)(2,1)S(1)} %collective-permute-done.1.refs_2_.refs_10_) | copy-start | bytes 786436
  30.9 11.6 %collective-permute-start.2 = (bf16[128,1024]{1,0:T(8,128)(2,1)S(1)}, bf16[128,1024]{1,0:T(8,128)(2,1)S(1)}, u32[]{:S(2)}, u32[]{:S(2)}) collective-permute-start(bf16[128,1024]{1,0:T(8,128)(2,1)S(1)} %collective-permute-done.1.refs_2_.refs_10_), channel_id=1, source_target_pairs={{0,4},{4,0},{8,12},{12,8},{16,20},{20,16},{24,28},{28,24},{1,5},{5... | collective-permute-start | bytes 786440 | tf_op jit(solution)/shard_map/ppermute | solution.py:829
  31.4 11.2 %copy-start.10 = (bf16[128,1024]{1,0:T(8,128)(2,1)}, bf16[128,1024]{1,0:T(8,128)(2,1)S(1)}, u32[]{:S(2)}) copy-start(bf16[128,1024]{1,0:T(8,128)(2,1)S(1)} %collective-permute-done.3.refs_4_.refs_12_) | copy-start | bytes 786436
  31.4 11.2 %collective-permute-start.4 = (bf16[128,1024]{1,0:T(8,128)(2,1)S(1)}, bf16[128,1024]{1,0:T(8,128)(2,1)S(1)}, u32[]{:S(2)}, u32[]{:S(2)}) collective-permute-start(bf16[128,1024]{1,0:T(8,128)(2,1)S(1)} %collective-permute-done.3.refs_4_.refs_12_), channel_id=1, source_target_pairs={{0,4},{4,0},{8,12},{12,8},{16,20},{20,16},{24,28},{28,24},{1,5},{5... | collective-permute-start | bytes 786440 | tf_op jit(solution)/shard_map/ppermute | solution.py:829
  35.0 7.6 %copy-start.11 = (bf16[128,1024]{1,0:T(8,128)(2,1)}, bf16[128,1024]{1,0:T(8,128)(2,1)S(1)}, u32[]{:S(2)}) copy-start(bf16[128,1024]{1,0:T(8,128)(2,1)S(1)} %collective-permute-done.5.refs_6_.refs_14_) | copy-start | bytes 786436
  35.0 7.6 %collective-permute-start.6 = (bf16[128,1024]{1,0:T(8,128)(2,1)S(1)}, bf16[128,1024]{1,0:T(8,128)(2,1)S(1)}, u32[]{:S(2)}, u32[]{:S(2)}) collective-permute-start(bf16[128,1024]{1,0:T(8,128)(2,1)S(1)} %collective-permute-done.5.refs_6_.refs_14_), channel_id=1, source_target_pairs={{0,4},{4,0},{8,12},{12,8},{16,20},{20,16},{24,28},{28,24},{1,5},{5... | collective-permute-start | bytes 786440 | tf_op jit(solution)/shard_map/ppermute | solution.py:829
  35.1 15.2 %copy-start.8 = (bf16[128,1024]{1,0:T(8,128)(2,1)S(1)}, bf16[128,1024]{1,0:T(8,128)(2,1)}, u32[]{:S(2)}) copy-start(bf16[128,1024]{1,0:T(8,128)(2,1)} %cot_ref.1) | copy-start | bytes 786436
  47.6 11.6 %collective-permute-start.7 = (bf16[8,128,128]{2,1,0:T(8,128)(2,1)}, bf16[8,128,128]{2,1,0:T(8,128)(2,1)S(1)}, u32[]{:S(2)}, u32[]{:S(2)}) collective-permute-start(bf16[8,128,128]{2,1,0:T(8,128)(2,1)} %get-tuple-element.100.refs_0_), channel_id=1, source_target_pairs={{0,3},{1,0},{2,1},{3,2},{4,7},{5,4},{6,5},{7,6},{8,11},{9,8},{10,9... | collective-permute-start | bytes 786440 | tf_op jit(solution)/shard_map/ppermute | solution.py:834
  48.1 11.7 %collective-permute-start.8 = (bf16[8,128,128]{2,1,0:T(8,128)(2,1)}, bf16[8,128,128]{2,1,0:T(8,128)(2,1)S(1)}, u32[]{:S(2)}, u32[]{:S(2)}) collective-permute-start(bf16[8,128,128]{2,1,0:T(8,128)(2,1)} %get-tuple-element.100.refs_0_), channel_id=1, source_target_pairs={{0,2},{1,3},{2,0},{3,1},{4,6},{5,7},{6,4},{7,5},{8,10},{9,11},{10,... | collective-permute-start | bytes 786440 | tf_op jit(solution)/shard_map/ppermute | solution.py:834
  50.2 12.5 %collective-permute-start.9 = (bf16[8,128,128]{2,1,0:T(8,128)(2,1)}, bf16[8,128,128]{2,1,0:T(8,128)(2,1)S(1)}, u32[]{:S(2)}, u32[]{:S(2)}) collective-permute-start(bf16[8,128,128]{2,1,0:T(8,128)(2,1)} %get-tuple-element.100.refs_0_), channel_id=1, source_target_pairs={{0,1},{1,2},{2,3},{3,0},{4,5},{5,6},{6,7},{7,4},{8,9},{9,10},{10,1... | collective-permute-start | bytes 786440 | tf_op jit(solution)/shard_map/ppermute | solution.py:834
  50.2 12.5 %collective-permute-start.10 = (bf16[128,1024]{1,0:T(8,128)(2,1)S(1)}, bf16[128,1024]{1,0:T(8,128)(2,1)S(1)}, u32[]{:S(2)}, u32[]{:S(2)}) collective-permute-start(bf16[128,1024]{1,0:T(8,128)(2,1)S(1)} %copy-done.8), channel_id=1, source_target_pairs={{0,24},{4,28},{8,0},{12,4},{16,8},{20,12},{24,16},{28,20},{1,25},{... | collective-permute-start | bytes 786440 | tf_op jit(solution)/shard_map/ppermute | solution.py:829
  53.1 9.6 %collective-permute-start.11 = (bf16[128,1024]{1,0:T(8,128)(2,1)S(1)}, bf16[128,1024]{1,0:T(8,128)(2,1)S(1)}, u32[]{:S(2)}, u32[]{:S(2)}) collective-permute-start(bf16[128,1024]{1,0:T(8,128)(2,1)S(1)} %copy-done.8), channel_id=1, source_target_pairs={{0,16},{4,20},{8,24},{12,28},{16,0},{20,4},{24,8},{28,12},{1,17},{... | collective-permute-start | bytes 786440 | tf_op jit(solution)/shard_map/ppermute | solution.py:829
  59.2 7.7 %copy-start.25 = (bf16[8,128,128]{2,1,0:T(8,128)(2,1)}, bf16[8,128,128]{2,1,0:T(8,128)(2,1)S(1)}, u32[]{:S(2)}) copy-start(bf16[8,128,128]{2,1,0:T(8,128)(2,1)S(1)} %collective-permute-done.7.refs_1_) | copy-start | bytes 786436
  59.2 7.6 %collective-permute-start.12 = (bf16[128,1024]{1,0:T(8,128)(2,1)S(1)}, bf16[128,1024]{1,0:T(8,128)(2,1)S(1)}, u32[]{:S(2)}, u32[]{:S(2)}) collective-permute-start(bf16[128,1024]{1,0:T(8,128)(2,1)S(1)} %copy-done.8), channel_id=1, source_target_pairs={{0,8},{4,12},{8,16},{12,20},{16,24},{20,28},{24,0},{28,4},{1,9},{5... | collective-permute-start | bytes 786440 | tf_op jit(solution)/shard_map/ppermute | solution.py:829
  59.8 7.1 %copy-start.26 = (bf16[8,128,128]{2,1,0:T(8,128)(2,1)}, bf16[8,128,128]{2,1,0:T(8,128)(2,1)S(1)}, u32[]{:S(2)}) copy-start(bf16[8,128,128]{2,1,0:T(8,128)(2,1)S(1)} %collective-permute-done.8.refs_2_) | copy-start | bytes 786436
  62.7 4.2 %copy-start.27 = (bf16[8,128,128]{2,1,0:T(8,128)(2,1)}, bf16[8,128,128]{2,1,0:T(8,128)(2,1)S(1)}, u32[]{:S(2)}) copy-start(bf16[8,128,128]{2,1,0:T(8,128)(2,1)S(1)} %collective-permute-done.9.refs_3_) | copy-start | bytes 786436
  66.9 28.7 %copy-start.7 = (bf16[4,128,1024]{2,1,0:T(8,128)(2,1)}, bf16[4,128,1024]{2,1,0:T(8,128)(2,1)S(1)}, u32[]{:S(2)}) copy-start(bf16[4,128,1024]{2,1,0:T(8,128)(2,1)S(1)} %pad_maximum_fusion.cot_ref) | copy-start | bytes 3145732
  80.5 8.7 %collective-permute-start.14 = (bf16[8,128,128]{2,1,0:T(8,128)(2,1)}, bf16[8,128,128]{2,1,0:T(8,128)(2,1)S(1)}, u32[]{:S(2)}, u32[]{:S(2)}) collective-permute-start(bf16[8,128,128]{2,1,0:T(8,128)(2,1)} %get-tuple-element.110.refs_0_), channel_id=1, source_target_pairs={{0,24},{4,28},{8,0},{12,4},{16,8},{20,12},{24,16},{28,20},{1,25},{... | collective-permute-start | bytes 786440 | tf_op jit(solution)/shard_map/ppermute | solution.py:829
  80.5 10.1 %collective-permute-start.16 = (bf16[8,128,128]{2,1,0:T(8,128)(2,1)}, bf16[8,128,128]{2,1,0:T(8,128)(2,1)S(1)}, u32[]{:S(2)}, u32[]{:S(2)}) collective-permute-start(bf16[8,128,128]{2,1,0:T(8,128)(2,1)} %get-tuple-element.110.refs_0_), channel_id=1, source_target_pairs={{0,16},{4,20},{8,24},{12,28},{16,0},{20,4},{24,8},{28,12},{1,17},{... | collective-permute-start | bytes 786440 | tf_op jit(solution)/shard_map/ppermute | solution.py:829
  81.4 11.9 %collective-permute-start.18 = (bf16[8,128,128]{2,1,0:T(8,128)(2,1)}, bf16[8,128,128]{2,1,0:T(8,128)(2,1)S(1)}, u32[]{:S(2)}, u32[]{:S(2)}) collective-permute-start(bf16[8,128,128]{2,1,0:T(8,128)(2,1)} %get-tuple-element.110.refs_0_), channel_id=1, source_target_pairs={{0,8},{4,12},{8,16},{12,20},{16,24},{20,28},{24,0},{28,4},{1,9},{5... | collective-permute-start | bytes 786440 | tf_op jit(solution)/shard_map/ppermute | solution.py:829
  82.6 10.8 %collective-permute-start.13 = (bf16[8,128,128]{2,1,0:T(8,128)(2,1)}, bf16[8,128,128]{2,1,0:T(8,128)(2,1)S(1)}, u32[]{:S(2)}, u32[]{:S(2)}) collective-permute-start(bf16[8,128,128]{2,1,0:T(8,128)(2,1)} %get-tuple-element.110.refs_0_), channel_id=1, source_target_pairs={{0,4},{4,0},{8,12},{12,8},{16,20},{20,16},{24,28},{28,24},{1,5},{5... | collective-permute-start | bytes 786440 | tf_op jit(solution)/shard_map/ppermute | solution.py:829
  89.2 6.5 %copy-start.28 = (bf16[8,128,128]{2,1,0:T(8,128)(2,1)}, bf16[8,128,128]{2,1,0:T(8,128)(2,1)S(1)}, u32[]{:S(2)}) copy-start(bf16[8,128,128]{2,1,0:T(8,128)(2,1)S(1)} %collective-permute-done.14.refs_2_) | copy-start | bytes 786436
  89.2 4.2 %collective-permute-start.15 = (bf16[8,128,128]{2,1,0:T(8,128)(2,1)S(1)}, bf16[8,128,128]{2,1,0:T(8,128)(2,1)S(1)}, u32[]{:S(2)}, u32[]{:S(2)}) collective-permute-start(bf16[8,128,128]{2,1,0:T(8,128)(2,1)S(1)} %collective-permute-done.14.refs_2_), channel_id=1, source_target_pairs={{0,4},{4,0},{8,12},{12,8},{16,20},{20,16},{24,28},{28,24},{1,5},{5... | collective-permute-start | bytes 786440 | tf_op jit(solution)/shard_map/ppermute | solution.py:829
  90.6 5.1 %copy-start.29 = (bf16[8,128,128]{2,1,0:T(8,128)(2,1)}, bf16[8,128,128]{2,1,0:T(8,128)(2,1)S(1)}, u32[]{:S(2)}) copy-start(bf16[8,128,128]{2,1,0:T(8,128)(2,1)S(1)} %collective-permute-done.16.refs_4_) | copy-start | bytes 786436
  90.6 2.7 %collective-permute-start.17 = (bf16[8,128,128]{2,1,0:T(8,128)(2,1)S(1)}, bf16[8,128,128]{2,1,0:T(8,128)(2,1)S(1)}, u32[]{:S(2)}, u32[]{:S(2)}) collective-permute-start(bf16[8,128,128]{2,1,0:T(8,128)(2,1)S(1)} %collective-permute-done.16.refs_4_), channel_id=1, source_target_pairs={{0,4},{4,0},{8,12},{12,8},{16,20},{20,16},{24,28},{28,24},{1,5},{5... | collective-permute-start | bytes 786440 | tf_op jit(solution)/shard_map/ppermute | solution.py:829
  93.4 2.4 copy-start.30
  93.4 1.5 collective-permute-start.19
  93.4 2.4 copy-start.31
  93.4 2.4 copy-start.32
  93.4 1.5 copy-start.33
  95.6 154.3 %reduce-scatter.2.cloned.1.call-start = ((), (), s32[]{:S(2)}) async-start(), calls=%async_computation.7 | async-start | bytes 13369344 | tf_op jit(solution)/shard_map/reduce_scatter | solution.py:960
  95.6 8.6 %collective-permute-start.20 = (bf16[4,128,1024]{2,1,0:T(8,128)(2,1)S(1)}, bf16[4,128,1024]{2,1,0:T(8,128)(2,1)S(1)}, u32[]{:S(2)}, u32[]{:S(2)}) collective-permute-start(bf16[4,128,1024]{2,1,0:T(8,128)(2,1)S(1)} %pad_maximum_fusion.cot_ref), channel_id=1, source_target_pairs={{0,4},{4,0},{8,12},{12,8},{16,20},{20,16},{24,28},{28,24},{1,5},{5... | collective-permute-start | bytes 3145736 | tf_op jit(solution)/shard_map/ppermute | solution.py:829
  104.2 1.0 copy-start.24
  138.2 1.3 copy-start.23
  138.2 4.2 %copy-start.5 = (bf16[4,128,1152]{2,1,0:T(8,128)(2,1)S(1)}, bf16[4,128,1152]{2,1,0:T(8,128)(2,1)}, u32[]{:S(2)}) copy-start(bf16[4,128,1152]{2,1,0:T(8,128)(2,1)} %get-tuple-element.128) | copy-start | bytes 3538948
  139.5 2.9 %collective-permute-start.21 = (bf16[4,128,1152]{2,1,0:T(8,128)(2,1)S(1)}, bf16[4,128,1152]{2,1,0:T(8,128)(2,1)S(1)}, u32[]{:S(2)}, u32[]{:S(2)}) collective-permute-start(bf16[4,128,1152]{2,1,0:T(8,128)(2,1)S(1)} %copy-done.23), channel_id=1, source_target_pairs={{0,4},{4,0},{8,12},{12,8},{16,20},{20,16},{24,28},{28,24},{1,5},{5... | collective-permute-start | bytes 3538952 | tf_op jit(solution)/shard_map/ppermute | solution.py:829
  143.5 16.8 %collective-permute-start.22 = (bf16[128,1152]{1,0:T(8,128)(2,1)S(1)}, bf16[128,1152]{1,0:T(8,128)(2,1)S(1)}, u32[]{:S(2)}, u32[]{:S(2)}) collective-permute-start(bf16[128,1152]{1,0:T(8,128)(2,1)S(1)} %get-tuple-element.178), channel_id=1, source_target_pairs={{0,8},{4,12},{8,16},{12,20},{16,24},{20,28},{24,0},{28,4},{1,9},{5... | collective-permute-start | bytes 884744 | tf_op jit(solution)/shard_map/ppermute | solution.py:829
  143.5 16.8 %collective-permute-start.23 = (bf16[128,1152]{1,0:T(8,128)(2,1)S(1)}, bf16[128,1152]{1,0:T(8,128)(2,1)S(1)}, u32[]{:S(2)}, u32[]{:S(2)}) collective-permute-start(bf16[128,1152]{1,0:T(8,128)(2,1)S(1)} %get-tuple-element.177), channel_id=1, source_target_pairs={{0,16},{4,20},{8,24},{12,28},{16,0},{20,4},{24,8},{28,12},{1,17},{... | collective-permute-start | bytes 884744 | tf_op jit(solution)/shard_map/ppermute | solution.py:829
  146.4 14.5 %collective-permute-start.24 = (bf16[128,1152]{1,0:T(8,128)(2,1)S(1)}, bf16[128,1152]{1,0:T(8,128)(2,1)S(1)}, u32[]{:S(2)}, u32[]{:S(2)}) collective-permute-start(bf16[128,1152]{1,0:T(8,128)(2,1)S(1)} %get-tuple-element.176), channel_id=1, source_target_pairs={{0,24},{4,28},{8,0},{12,4},{16,8},{20,12},{24,16},{28,20},{1,25},{... | collective-permute-start | bytes 884744 | tf_op jit(solution)/shard_map/ppermute | solution.py:829
  161.6 8.5 %copy-start.6 = (bf16[4,128,1024]{2,1,0:T(8,128)(2,1)S(1)}, bf16[4,128,1024]{2,1,0:T(8,128)(2,1)}, u32[]{:S(2)}) copy-start(bf16[4,128,1024]{2,1,0:T(8,128)(2,1)} %get-tuple-element.138) | copy-start | bytes 3145732
  166.4 3.7 %collective-permute-start.25 = (bf16[4,128,1024]{2,1,0:T(8,128)(2,1)}, bf16[4,128,1024]{2,1,0:T(8,128)(2,1)S(1)}, u32[]{:S(2)}, u32[]{:S(2)}) collective-permute-start(bf16[4,128,1024]{2,1,0:T(8,128)(2,1)} %get-tuple-element.139), channel_id=1, source_target_pairs={{0,4},{4,0},{8,12},{12,8},{16,20},{20,16},{24,28},{28,24},{1,5},{5... | collective-permute-start | bytes 3145736 | tf_op jit(solution)/shard_map/ppermute | solution.py:829
  166.4 14.6 %all-to-all-start.2 = ((bf16[8,128,256]{2,1,0:T(8,128)(2,1)}), bf16[8,128,256]{2,1,0:T(8,128)(2,1)S(1)}, u32[]{:S(2)}, u32[]{:S(2)}) async-start(bf16[8,128,256]{2,1,0:T(8,128)(2,1)} %get-tuple-element.133), calls=%async_computation.2 | async-start | bytes 1048576 | tf_op jit(solution)/shard_map/all_to_all | solution.py:972
  171.3 27.5 %collective-permute-start.26 = (bf16[128,1024]{1,0:T(8,128)(2,1)}, bf16[128,1024]{1,0:T(8,128)(2,1)S(1)}, u32[]{:S(2)}, u32[]{:S(2)}) collective-permute-start(bf16[128,1024]{1,0:T(8,128)(2,1)} %get-tuple-element.182), channel_id=1, source_target_pairs={{0,8},{4,12},{8,16},{12,20},{16,24},{20,28},{24,0},{28,4},{1,9},{5... | collective-permute-start | bytes 786440 | tf_op jit(solution)/shard_map/ppermute | solution.py:829
  173.4 25.5 %collective-permute-start.27 = (bf16[128,1024]{1,0:T(8,128)(2,1)}, bf16[128,1024]{1,0:T(8,128)(2,1)S(1)}, u32[]{:S(2)}, u32[]{:S(2)}) collective-permute-start(bf16[128,1024]{1,0:T(8,128)(2,1)} %get-tuple-element.181), channel_id=1, source_target_pairs={{0,16},{4,20},{8,24},{12,28},{16,0},{20,4},{24,8},{28,12},{1,17},{... | collective-permute-start | bytes 786440 | tf_op jit(solution)/shard_map/ppermute | solution.py:829
  176.0 22.8 %collective-permute-start.28 = (bf16[128,1024]{1,0:T(8,128)(2,1)S(1)}, bf16[128,1024]{1,0:T(8,128)(2,1)S(1)}, u32[]{:S(2)}, u32[]{:S(2)}) collective-permute-start(bf16[128,1024]{1,0:T(8,128)(2,1)S(1)} %get-tuple-element.180), channel_id=1, source_target_pairs={{0,24},{4,28},{8,0},{12,4},{16,8},{20,12},{24,16},{28,20},{1,25},{... | collective-permute-start | bytes 786440 | tf_op jit(solution)/shard_map/ppermute | solution.py:829
  198.9 13.8 %collective-permute-start.29 = (bf16[8,128,128]{2,1,0:T(8,128)(2,1)}, bf16[8,128,128]{2,1,0:T(8,128)(2,1)S(1)}, u32[]{:S(2)}, u32[]{:S(2)}) collective-permute-start(bf16[8,128,128]{2,1,0:T(8,128)(2,1)} %get-tuple-element.144), channel_id=1, source_target_pairs={{0,1},{1,2},{2,3},{3,0},{4,5},{5,6},{6,7},{7,4},{8,9},{9,10},{10,1... | collective-permute-start | bytes 786440 | tf_op jit(solution)/shard_map/ppermute | solution.py:834
  199.1 19.9 %collective-permute-start.30 = (bf16[8,128,128]{2,1,0:T(8,128)(2,1)}, bf16[8,128,128]{2,1,0:T(8,128)(2,1)S(1)}, u32[]{:S(2)}, u32[]{:S(2)}) collective-permute-start(bf16[8,128,128]{2,1,0:T(8,128)(2,1)} %get-tuple-element.154), channel_id=1, source_target_pairs={{0,2},{1,3},{2,0},{3,1},{4,6},{5,7},{6,4},{7,5},{8,10},{9,11},{10,... | collective-permute-start | bytes 786440 | tf_op jit(solution)/shard_map/ppermute | solution.py:834
  204.1 14.9 %collective-permute-start.31 = (bf16[8,128,128]{2,1,0:T(8,128)(2,1)}, bf16[8,128,128]{2,1,0:T(8,128)(2,1)S(1)}, u32[]{:S(2)}, u32[]{:S(2)}) collective-permute-start(bf16[8,128,128]{2,1,0:T(8,128)(2,1)} %get-tuple-element.155), channel_id=1, source_target_pairs={{0,3},{1,0},{2,1},{3,2},{4,7},{5,4},{6,5},{7,6},{8,11},{9,8},{10,9... | collective-permute-start | bytes 786440 | tf_op jit(solution)/shard_map/ppermute | solution.py:834
  212.6 5.1 %copy-start.19 = (bf16[8,128,128]{2,1,0:T(8,128)(2,1)}, bf16[8,128,128]{2,1,0:T(8,128)(2,1)S(1)}, u32[]{:S(2)}) copy-start(bf16[8,128,128]{2,1,0:T(8,128)(2,1)S(1)} %collective-permute-done.29.refs_1_) | copy-start | bytes 786436
  223.1 14.5 %all-to-all-start.4 = ((bf16[8,128,256]{2,1,0:T(8,128)(2,1)}), bf16[8,128,256]{2,1,0:T(8,128)(2,1)S(1)}, u32[]{:S(2)}, u32[]{:S(2)}) async-start(bf16[8,128,256]{2,1,0:T(8,128)(2,1)} %get-tuple-element.159), calls=%async_computation.4 | async-start | bytes 1048576 | tf_op jit(solution)/shard_map/all_to_all | solution.py:983
  230.6 13.5 %copy-start.2 = (f32[128,1024]{1,0:T(8,128)S(1)}, f32[128,1024]{1,0:T(8,128)}, u32[]{:S(2)}) copy-start(f32[128,1024]{1,0:T(8,128)} %get-tuple-element.118.mid_ref) | copy-start | bytes 1572868
  237.6 7.4 %copy-start.4 = (bf16[8,128,256]{2,1,0:T(8,128)(2,1)}, bf16[8,128,256]{2,1,0:T(8,128)(2,1)S(1)}, u32[]{:S(2)}) copy-start(bf16[8,128,256]{2,1,0:T(8,128)(2,1)S(1)} %all-to-all-done.4.got_ref) | copy-start | bytes 1572868
  237.6 25.3 %all-to-all-start.3 = ((bf16[128,8,512]{2,1,0:T(8,128)(2,1)}), bf16[128,8,512]{2,1,0:T(8,128)(2,1)S(1)}, u32[]{:S(2)}, u32[]{:S(2)}) async-start(bf16[128,8,512]{2,1,0:T(8,128)(2,1)} %bitcast.40), calls=%async_computation.3 | async-start | bytes 2097152 | tf_op jit(solution)/shard_map/all_to_all | solution.py:986
  249.9 2.2 copy-start.1
  262.9 1.0 copy-start
  (11 other events, 8.4 us)
Sparse Core Ops, SparseCore 0:
  11.5 75.9 all-gather.3
  95.0 35.6 all-gather.5
  138.4 106.7 reduce-scatter.1
